TPU v7x, 32 devices: a whole 2x2x4 slice. The times are simulated.
32 devices in a mesh: band: 2 (over x), gy: 4 (over y, core), gz: 4 (over z).
Axes of the slice: x: 2, y: 2, z: 4, core: 2. Of those that a mesh axis runs over, the one named last changes fastest.
Arguments:
- orbitals: bfloat16 [4, 128, 128, 256], P('band', 'gy', 'gz'), may hold values from -6 to 6
- potential: float32 [128, 128, 128], P(('gy', 'gz')), may hold values from -6 to 6
- cutoff_mask: int32 [128, 128, 128], P('gy', 'gz'), may hold values from 0 to 1, as said below
- channels: bfloat16 [4, 128, 128, 128], P(None, 'gy', 'gz'), may hold values from -0.125 to 0.125
- positions: float32 [8, 3], replicated, may hold values from 0 to 1
- proj_atom: int32 [32], replicated, may hold values from 0 to 7
- proj_chan: int32 [32], replicated, may hold values from 0 to 3
- coupling: float32 [32], replicated, may hold values from 0.5 to 2
- occupations: float32 [4], P('band'), may hold values from 0.25 to 0.75
Outputs:
- applied: bfloat16 [4, 128, 128, 256], P('band', 'gy', 'gz')
- density: float32 [128, 128, 128], P(('gy', 'gz'))
Inputs may be any that keep to these rules, and one draw needn't show every extreme that they name: With s = f(ky)^2 + f(kz)^2 + f(kx)^2, cutoff_mask is 1 wherever s < 56^2 and 0 wherever s >= 128^2 / 4; in between each plane wave's value is its own.
All inputs are finite; a program needn't handle non-finite values.
Results may differ from a plain program's by a relative error of at most 0.018.
Values may be sent and summed in bfloat16 or wider, within the bound.
A program may use at most 128 MiB of HBM per device.

v0:
```python
import math

import jax
import jax.numpy as jnp
from jax import lax
from jax.sharding import PartitionSpec as P

kinetic_scale = 1.0 / 1024.0


def dft_table(length, sign_value):
    grid_index = jnp.arange(length, dtype=jnp.int32)
    product = grid_index[:, None] * grid_index[None, :] % length
    phase_angle = 2.0 * math.pi / length * product.astype(jnp.float32)
    cosine_part = jnp.cos(phase_angle) / math.sqrt(length)
    sine_part = sign_value * jnp.sin(phase_angle) / math.sqrt(length)
    upper_rows = jnp.stack([cosine_part, -sine_part], axis=1)
    lower_rows = jnp.stack([sine_part, cosine_part], axis=1)
    return jnp.stack([upper_rows, lower_rows], axis=0).astype(jnp.bfloat16)


def frequencies(first_index, span, length):
    grid_index = first_index + jnp.arange(span, dtype=jnp.int32)
    return jnp.where(grid_index >= length // 2, grid_index - length, grid_index).astype(jnp.float32)


def axis_phase(coordinate, freq):
    phase_angle = 2.0 * math.pi * (coordinate[:, None] * freq[None, :])
    return (jnp.cos(phase_angle), jnp.sin(phase_angle))


def projector_parts(channels, positions, atom_ids, kind_ids, freq_y, freq_z, freq_x):
    atom_hot = (
        atom_ids[:, None] == jnp.arange(positions.shape[0], dtype=jnp.int32)[None, :]
    ).astype(jnp.float32)
    located = jnp.dot(atom_hot, positions, precision=lax.Precision.HIGHEST)
    kind_hot = (
        kind_ids[:, None] == jnp.arange(channels.shape[0], dtype=jnp.int32)[None, :]
    ).astype(jnp.bfloat16)
    radial = jnp.einsum("bc,cyzx->byzx", kind_hot, channels, preferred_element_type=jnp.float32)
    cos_y, sin_y = axis_phase(located[:, 1], freq_y)
    cos_z, sin_z = axis_phase(located[:, 2], freq_z)
    cos_x, sin_x = axis_phase(located[:, 0], freq_x)
    cos_yz = cos_y[:, :, None] * cos_z[:, None, :] - sin_y[:, :, None] * sin_z[:, None, :]
    sin_yz = sin_y[:, :, None] * cos_z[:, None, :] + cos_y[:, :, None] * sin_z[:, None, :]
    cosine = (
        cos_yz[..., None] * cos_x[:, None, None, :] - sin_yz[..., None] * sin_x[:, None, None, :]
    )
    sine = sin_yz[..., None] * cos_x[:, None, None, :] + cos_yz[..., None] * sin_x[:, None, None, :]
    real_beta = (radial * cosine).astype(jnp.bfloat16)
    imag_beta = (-(radial * sine)).astype(jnp.bfloat16)
    return (real_beta, imag_beta)


def shards(
    orbitals,
    potential,
    cutoff_mask,
    channels,
    positions,
    proj_atom,
    proj_chan,
    coupling,
    occupations,
):
    orbit_count = orbitals.shape[0]
    rows_y = orbitals.shape[1]
    rows_z = orbitals.shape[2]
    length = orbitals.shape[3] // 2
    parts_y = lax.axis_size("gy")
    parts_z = lax.axis_size("gz")
    thin_x = length // (parts_y * parts_z)
    inverse = dft_table(length, 1.0)
    forward = dft_table(length, -1.0)
    inv_x = jnp.transpose(inverse, (2, 3, 0, 1)).reshape(2 * length, 2, parts_y, parts_z, thin_x)
    fwd_x = jnp.transpose(forward, (2, 3, 0, 1)).reshape(2, parts_y, parts_z, thin_x, 2 * length)
    mask_full = jnp.concatenate([cutoff_mask, cutoff_mask], axis=2) != 0
    masked = jnp.where(mask_full[None], orbitals, jnp.zeros_like(orbitals))
    freq_y = frequencies(lax.axis_index("gy") * rows_y, rows_y, length)
    freq_z = frequencies(lax.axis_index("gz") * rows_z, rows_z, length)
    freq_x = frequencies(0, length, length)
    real_orbs = masked[..., :length]
    imag_orbs = masked[..., length:]
    real_beta, imag_beta = projector_parts(
        channels, positions, proj_atom, proj_chan, freq_y, freq_z, freq_x
    )
    real_over = jnp.einsum(
        "pyzx,nyzx->pn", real_beta, real_orbs, preferred_element_type=jnp.float32
    )
    real_over = real_over + jnp.einsum(
        "pyzx,nyzx->pn", imag_beta, imag_orbs, preferred_element_type=jnp.float32
    )
    imag_over = jnp.einsum(
        "pyzx,nyzx->pn", real_beta, imag_orbs, preferred_element_type=jnp.float32
    )
    imag_over = imag_over - jnp.einsum(
        "pyzx,nyzx->pn", imag_beta, real_orbs, preferred_element_type=jnp.float32
    )
    partial_intersections = jnp.stack([real_over, imag_over], axis=0)
    intersections = lax.psum(partial_intersections, ("gy", "gz"))
    spread = jnp.einsum(
        "nyzk,kcpqx->npqcxyz", masked, inv_x, preferred_element_type=jnp.float32
    ).astype(jnp.bfloat16)
    spread = spread.reshape(orbit_count, parts_y, parts_z, 2, thin_x, rows_y * rows_z)
    arrived = lax.all_to_all(
        lax.all_to_all(spread, "gy", split_axis=1, concat_axis=5, tiled=True),
        "gz",
        split_axis=2,
        concat_axis=5,
        tiled=True,
    )
    arrived = arrived.reshape(orbit_count, 2, thin_x, parts_z, length, rows_z)
    rotated = jnp.einsum(
        "ncxqyz,ducy->ndxqzu", arrived, inverse, preferred_element_type=jnp.float32
    ).astype(jnp.bfloat16)
    rotated = rotated.reshape(orbit_count, 2, thin_x, length, length)
    real_field = jnp.einsum(
        "ndxzu,fwdz->nfxuw", rotated, inverse, preferred_element_type=jnp.float32
    )
    partial_density = jnp.sum(
        occupations[:, None, None, None] * jnp.sum(real_field * real_field, axis=1), axis=0
    )
    density = lax.psum(partial_density.astype(jnp.bfloat16), "band").astype(jnp.float32)
    scaled = (potential[None, None] * real_field).astype(jnp.bfloat16)
    back_z = jnp.einsum(
        "nfxuw,dzfw->ndxuz", scaled, forward, preferred_element_type=jnp.float32
    ).astype(jnp.bfloat16)
    folded = jnp.einsum(
        "ndxuz,cydu->ncxyz", back_z, forward, preferred_element_type=jnp.float32
    ).astype(jnp.bfloat16)
    folded = folded.reshape(orbit_count, 1, 1, 2, thin_x, length, length)
    returned = lax.all_to_all(
        lax.all_to_all(folded, "gy", split_axis=5, concat_axis=1, tiled=True),
        "gz",
        split_axis=6,
        concat_axis=2,
        tiled=True,
    )
    local_g = jnp.einsum("npqcxyz,cpqxk->nyzk", returned, fwd_x, preferred_element_type=jnp.float32)
    coefficients = (intersections * coupling[None, :, None]).astype(jnp.bfloat16)
    coef_real = coefficients[0]
    coef_imag = coefficients[1]
    real_sum = jnp.einsum("pn,pyzx->nyzx", coef_real, real_beta, preferred_element_type=jnp.float32)
    real_sum = real_sum - jnp.einsum(
        "pn,pyzx->nyzx", coef_imag, imag_beta, preferred_element_type=jnp.float32
    )
    imag_sum = jnp.einsum("pn,pyzx->nyzx", coef_imag, real_beta, preferred_element_type=jnp.float32)
    imag_sum = imag_sum + jnp.einsum(
        "pn,pyzx->nyzx", coef_real, imag_beta, preferred_element_type=jnp.float32
    )
    nonlocal_part = jnp.concatenate([real_sum, imag_sum], axis=3)
    energy = (
        kinetic_scale
        * 0.5
        * (freq_y[:, None, None] ** 2 + freq_z[None, :, None] ** 2 + freq_x[None, None, :] ** 2)
    )
    energy = jnp.concatenate([energy, energy], axis=2)
    total = energy[None] * masked.astype(jnp.float32) + local_g + nonlocal_part
    applied = jnp.where(mask_full[None], total, jnp.zeros_like(total)).astype(jnp.bfloat16)
    return (applied, density)


def solution(mesh):
    placed = (
        P("band", "gy", "gz", None),
        P(("gy", "gz"), None, None),
        P("gy", "gz", None),
        P(None, "gy", "gz", None),
        P(),
        P(),
        P(),
        P(),
        P("band"),
    )
    return jax.shard_map(
        shards,
        mesh=mesh,
        in_specs=placed,
        out_specs=(P("band", "gy", "gz", None), P(("gy", "gz"), None, None)),
        check_vma=False,
    )
```

profile of v0, /device:TPU:1, one launch (start us, length us, event | category | flops | bytes accessed | tf_op | source)
XLA Modules:
  0.0 244.6 jit_solution(5139031643998467622)
XLA Ops:
  7.5 0.3 multiply_convert_fusion.1
  8.0 1.4 add_compare_fusion
  9.4 0.7 fusion.42
  10.3 1.4 broadcast_select_fusion
  11.7 1.3 convert_bitcast_fusion
  13.0 3.2 %copy.117 = bf16[2,4,4,2,8,32,32]{6,5,4,3,2,0,1:T(8,128)(2,1)} copy(bf16[2,4,4,2,8,32,32]{6,4,5,0,2,1,3:T(8,128)(2,1)S(1)} %convert_bitcast_fusion) | data formatting | bytes 2097152 | tf_op jit(solution)/shard_map/reshape | solution.py:104
  16.2 7.0 %reshape.426 = bf16[2,4,4,2,8,1024]{5,4,3,2,0,1:T(8,128)(2,1)} reshape(bf16[2,4,4,2,8,32,32]{6,5,4,3,2,0,1:T(8,128)(2,1)} %copy.117) | data formatting | bytes 2097152 | tf_op jit(solution)/shard_map/reshape | solution.py:104
  23.2 4.3 %all-to-all-start = ((bf16[2,4,4,2,8,1024]{5,4,3,2,0,1:T(8,128)(2,1)}), bf16[2,4,4,2,8,1024]{5,4,3,2,0,1:T(8,128)(2,1)S(1)}, u32[]{:S(2)}, u32[]{:S(2)}) async-start(bf16[2,4,4,2,8,1024]{5,4,3,2,0,1:T(8,128)(2,1)} %reshape.426), calls=%async_computation | async-start | bytes 2097152 | tf_op jit(solution)/shard_map/all_to_all | solution.py:106
  27.5 1.2 fusion.77
  28.9 0.6 fusion.63
  29.6 0.9 fusion.55
  30.7 13.7 %multiply_convert_fusion = (bf16[32,32,32,128]{3,0,2,1:T(8,128)(2,1)S(1)}, bf16[32,32,32,128]{3,0,2,1:T(8,128)(2,1)S(1)}) fusion(f32[32,128]{1,0:T(8,128)S(1)} %get-tuple-element.20, f32[32,32,32]{0,2,1:T(8,128)S(1)} %get-tuple-element.11, f32[32,128]{1,0:T(8,128)S(1)} %get-tuple-element.19, f32[32,32,32]{0,2,1:T(8,128)S(1)} %get-tuple-element.10, ...), kind=kOutput, calls=%fused_computation.1 | convolution fusion | flops 79691904 | bytes 18120832 | tf_op jit(solution)/shard_map/bc,cyzx->byzx/dot_general | solution.py:40
  44.4 2.3 convolution_bitcast_fusion.3
  46.7 2.3 fusion.17
  48.9 1.3 copy-done.3
  50.2 2.3 convolution_bitcast_fusion.1
  52.5 1.0 copy.68
  53.5 5.7 %fusion.15 = f32[1,32,2]{1,2,0:T(2,128)S(1)} fusion(f32[32,2]{0,1:T(2,128)S(1)} %convolution_bitcast_fusion.1, bf16[32,32,32,128]{3,0,2,1:T(8,128)(2,1)} %copy-done.2, bf16[2,32,32,128]{3,2,1,0:T(8,128)(2,1)S(1)} %copy-done.8), kind=kOutput, calls=%fused_computation.22 | convolution fusion | flops 16777280 | bytes 8913408 | tf_op jit(solution)/shard_map/pyzx,nyzx->pn/dot_general | solution.py:96
  59.2 31.6 %psum.14 = f32[2,32,2]{1,2,0:T(2,128)S(1)} all-reduce(f32[2,32,2]{1,2,0:T(2,128)S(1)} %pad_maximum_fusion.11), channel_id=1, replica_groups=mesh['band'=2,'gy'=4,'gz'=4] {'gy','gz'}, use_global_device_ids=true, to_apply=%region_0.1 | all-reduce | flops 128 | bytes 1024 | tf_op jit(solution)/shard_map/psum | solution.py:100
  90.8 0.9 copy.118
  91.7 1.6 reshape.427
  93.3 3.7 %all-to-all-start.1 = ((bf16[2,1,4,2,8,4096]{5,4,3,0,1,2:T(8,128)(2,1)}), bf16[2,1,4,2,8,4096]{5,4,3,0,1,2:T(8,128)(2,1)S(1)}, u32[]{:S(2)}, u32[]{:S(2)}) async-start(bf16[2,1,4,2,8,4096]{5,4,3,0,1,2:T(8,128)(2,1)} %reshape.427), calls=%async_computation.1 | async-start | bytes 2097152 | tf_op jit(solution)/shard_map/all_to_all | solution.py:105
  97.4 1.1 pad_maximum_fusion
  98.5 4.6 %fusion.67 = f32[2,32,32,128]{3,0,2,1:T(2,128)S(1)} fusion(bf16[32,32,32,128]{3,0,2,1:T(8,128)(2,1)} %copy-done.3, bf16[2,32,2]{1,2,0:T(2,128)(2,1)S(1)} %multiply_convert_fusion.4), kind=kOutput, calls=%fused_computation.112 | convolution fusion | flops 16777216 | bytes 9437696 | tf_op jit(solution)/shard_map/pn,pyzx->nyzx/dot_general | solution.py:143
  103.0 18.8 %all-to-all-done.1 = bf16[2,1,4,2,8,4096]{5,4,3,0,1,2:T(8,128)(2,1)S(1)} async-done(((bf16[2,1,4,2,8,4096]{5,4,3,0,1,2:T(8,128)(2,1)}), bf16[2,1,4,2,8,4096]{5,4,3,0,1,2:T(8,128)(2,1)S(1)}, u32[]{:S(2)}, u32[]{:S(2)}) %all-to-all-start.1) | async-done | bytes 1048608 | tf_op jit(solution)/shard_map/all_to_all | solution.py:105
  121.8 4.4 %reshape.428 = bf16[2,2,8,4,128,32]{5,4,2,1,0,3:T(8,128)(2,1)} reshape(bf16[2,1,1,2,8,4,4096]{6,4,3,0,5,2,1:T(8,128)(2,1)S(1)} %bitcast.203) | data formatting | bytes 2097152 | tf_op jit(solution)/shard_map/reshape | solution.py:112
  126.2 3.4 %bitcast_convert_fusion.2 = bf16[2,128,2,8,4,32]{1,5,4,3,2,0:T(8,128)(2,1)S(1)} fusion(bf16[1,128,2,128]{3,1,2,0:T(8,128)(2,1)S(1)} %get-tuple-element.13, bf16[1,128,2,128]{3,1,2,0:T(8,128)(2,1)S(1)} %get-tuple-element.14, bf16[2,2,8,4,128,32]{5,4,2,1,0,3:T(8,128)(2,1)} %reshape.428), kind=kOutput, calls=%fused_computation.17 | convolution fusion | flops 269221888 | bytes 2228224 | tf_op jit(solution)/shard_map/ncxqyz,ducy->ndxqzu/dot_general | solution.py:113
  129.7 3.6 %fusion.7 = (f32[2,8,128,128]{2,3,1,0:T(8,128)}, bf16[2,2,8,128,128,1]{3,4,2,0,1,5:T(8,128)(2,1)}) fusion(f32[8,128,128]{1,2,0:T(8,128)} %copy.68, bf16[2,2,8,128,128]{4,3,2,0,1:T(8,128)(2,1)S(1)} %bitcast.206, bf16[1,128,2,128]{3,1,2,0:T(8,128)(2,1)S(1)} %get-tuple-element.13, bf16[1,128,2,128]{3,1,2,0:T(8,128)(2,1)S(1)} %get-tuple-element.14), kind=kOutput, calls=%fused_computation.14 | convolution fusion | flops 270532608 | bytes 3801088 | tf_op jit(solution)/shard_map/ndxzu,fwdz->nfxuw/dot_general | solution.py:117
  133.2 2.1 fusion.13
  135.3 1.7 copy.79
  137.0 5.1 %all-to-all-start.2 = ((bf16[2,1,1,2,8,128,128]{6,4,0,3,2,1,5:T(8,128)(2,1)}), bf16[2,1,1,2,8,128,128]{6,4,0,3,2,1,5:T(8,128)(2,1)S(1)}, u32[]{:S(2)}, u32[]{:S(2)}) async-start(bf16[2,1,1,2,8,128,128]{6,4,0,3,2,1,5:T(8,128)(2,1)} %copy.79), calls=%async_computation.2 | async-start | bytes 2097152 | tf_op jit(solution)/shard_map/all_to_all | solution.py:133
  142.2 4.6 %fusion.69 = f32[2,32,32,128]{3,0,2,1:T(2,128)S(1)} fusion(bf16[32,32,32,128]{3,0,2,1:T(8,128)(2,1)} %copy-done.2, bf16[2,32,2]{1,2,0:T(2,128)(2,1)S(1)} %multiply_convert_fusion.4), kind=kOutput, calls=%fused_computation.114 | convolution fusion | flops 16777216 | bytes 9437696 | tf_op jit(solution)/shard_map/pn,pyzx->nyzx/dot_general | solution.py:144
  146.7 1.1 copy_subtract_fusion
  147.9 7.9 %all-to-all-done.2 = bf16[2,1,1,2,8,128,128]{6,4,0,3,2,1,5:T(8,128)(2,1)S(1)} async-done(((bf16[2,1,1,2,8,128,128]{6,4,0,3,2,1,5:T(8,128)(2,1)}), bf16[2,1,1,2,8,128,128]{6,4,0,3,2,1,5:T(8,128)(2,1)S(1)}, u32[]{:S(2)}, u32[]{:S(2)}) %all-to-all-start.2) | async-done | bytes 1048608 | tf_op jit(solution)/shard_map/all_to_all | solution.py:133
  155.8 7.4 %copy.80 = bf16[2,1,1,2,8,4,32,128]{6,4,3,5,0,7,2,1:T(8,128)(2,1)} copy(bf16[2,1,1,2,8,4,32,128]{7,4,0,3,6,5,2,1:T(8,128)(2,1)S(1)} %bitcast.204) | data formatting | bytes 2097152 | tf_op jit(solution)/shard_map/all_to_all | solution.py:133
  163.2 6.0 %bitcast_bitcast_fusion = bf16[128,1,2,4,2,8,32]{6,5,4,3,2,1,0:T(8,128)(2,1)} fusion(bf16[2,1,1,2,8,4,32,128]{6,4,3,5,0,7,2,1:T(8,128)(2,1)} %copy.80), kind=kLoop, calls=%fused_computation.122 | loop fusion | bytes 2097152
  169.2 6.4 %reshape.429 = bf16[4,2,65536]{2,1,0:T(2,128)(2,1)} reshape(bf16[128,1,2,4,2,8,32]{6,5,4,3,2,1,0:T(8,128)(2,1)} %bitcast_bitcast_fusion) | data formatting | bytes 2097152
  175.6 4.2 %all-to-all-start.3 = ((bf16[4,2,65536]{2,1,0:T(2,128)(2,1)}), bf16[4,2,65536]{2,1,0:T(2,128)(2,1)}, u32[]{:S(2)}, u32[]{:S(2)}) async-start(bf16[4,2,65536]{2,1,0:T(2,128)(2,1)} %reshape.429), calls=%async_computation.3 | async-start | bytes 2097152 | tf_op jit(solution)/shard_map/all_to_all | solution.py:132
  179.8 0.3 all-reduce.2.cloned.1.call-start
  180.4 4.7 %fusion.68 = f32[2,32,32,128]{3,0,2,1:T(2,128)S(1)} fusion(bf16[32,32,32,128]{3,0,2,1:T(8,128)(2,1)} %copy-done.3, bf16[2,32,2]{1,2,0:T(2,128)(2,1)S(1)} %multiply_convert_fusion.4), kind=kOutput, calls=%fused_computation.113 | convolution fusion | flops 16777216 | bytes 9437696 | tf_op jit(solution)/shard_map/pn,pyzx->nyzx/dot_general | solution.py:147
  185.1 4.6 %fusion.66 = f32[2,32,32,128]{3,0,2,1:T(2,128)S(1)} fusion(bf16[32,32,32,128]{3,0,2,1:T(8,128)(2,1)} %copy-done.2, bf16[2,32,2]{1,2,0:T(2,128)(2,1)S(1)} %multiply_convert_fusion.4), kind=kOutput, calls=%fused_computation.111 | convolution fusion | flops 16777216 | bytes 9437696 | tf_op jit(solution)/shard_map/pn,pyzx->nyzx/dot_general | solution.py:148
  189.7 0.9 multiply_reduce_fusion
  190.6 1.1 copy_add_fusion
  191.7 22.1 %all-reduce.2.cloned.1.call-done = bf16[8,128,128]{1,2,0:T(8,128)(2,1)} async-done(((bf16[8,128,128]{1,2,0:T(8,128)(2,1)}), bf16[8,128,128]{1,2,0:T(8,128)(2,1)}) %all-reduce.2.cloned.1.call-update) | async-done | bytes 262160 | tf_op jit(solution)/shard_map/psum | solution.py:123
  213.8 1.9 copy.94
  215.7 5.2 %reshape.430 = bf16[128,1,2,4,2,8,32]{6,5,4,3,2,1,0:T(8,128)(2,1)} reshape(bf16[4,2,65536]{2,1,0:T(2,128)(2,1)} %all-to-all-done.3) | data formatting | bytes 2097152
  220.9 10.4 %copy.82 = bf16[2,4,1,2,8,32,4,32]{7,6,4,5,0,1,3,2:T(4,128)(2,1)} copy(bf16[2,4,1,2,8,32,4,32]{5,4,3,1,0,7,6,2:T(8,128)(2,1)} %bitcast.202) | data formatting | bytes 2097152 | tf_op jit(solution)/shard_map/all_to_all | solution.py:132
  231.3 6.5 %fusion.5 = bf16[2,32,32,256]{3,2,1,0:T(8,128)(2,1)} fusion(f32[2,32,32,128]{3,2,1,0:T(8,128)} %copy_add_fusion, f32[2,32,32,128]{3,2,1,0:T(8,128)S(1)} %copy-done.5, bf16[2,32,32,256]{3,2,1,0:T(8,128)(2,1)S(1)} %broadcast_select_fusion, bf16[2,4,1,2,8,32,4,32]{7,6,4,5,0,1,3,2:T(4,128)(2,1)} %copy.82, f32[32,32,256]{2,1,0:T(8,128)} %pad_maximum_fusion, ...), kind=kOutput, calls=%fused_computation.9 | convolution fusion | flops 272105472 | bytes 6684672 | tf_op jit(solution)/shard_map/npqcxyz,cpqxk->nyzk/dot_general | solution.py:139
  (54 shorter events, 1.9 us)
Async XLA Ops:
  7.2 23.5 %copy-start = (bf16[4,32,32,128]{3,2,1,0:T(8,128)(2,1)S(1)}, bf16[4,32,32,128]{3,2,1,0:T(8,128)(2,1)}, u32[]{:S(2)}) copy-start(bf16[4,32,32,128]{3,2,1,0:T(8,128)(2,1)} %param.12) | copy-start | bytes 3145732
  13.0 15.7 %copy-start.14 = (f32[8,3]{0,1:T(4,128)S(1)}, f32[8,3]{0,1:T(4,128)}, u32[]{:S(2)}) copy-start(f32[8,3]{0,1:T(4,128)} %param.13) | copy-start | bytes 292
  13.0 15.7 %copy-start.15 = (s32[32]{0:T(128)S(1)}, s32[32]{0:T(128)}, u32[]{:S(2)}) copy-start(s32[32]{0:T(128)} %param.14) | copy-start | bytes 388
  23.2 67.6 %all-to-all-start = ((bf16[2,4,4,2,8,1024]{5,4,3,2,0,1:T(8,128)(2,1)}), bf16[2,4,4,2,8,1024]{5,4,3,2,0,1:T(8,128)(2,1)S(1)}, u32[]{:S(2)}, u32[]{:S(2)}) async-start(bf16[2,4,4,2,8,1024]{5,4,3,2,0,1:T(8,128)(2,1)} %reshape.426), calls=%async_computation | async-start | bytes 2097152 | tf_op jit(solution)/shard_map/all_to_all | solution.py:106
  30.7 13.7 %copy-start.7 = (bf16[2,32,32,128]{3,2,1,0:T(8,128)(2,1)S(1)}, bf16[2,32,32,128]{3,2,1,0:T(8,128)(2,1)}, u32[]{:S(2)}) copy-start(bf16[2,32,32,128]{3,2,1,0:T(8,128)(2,1)} %get-tuple-element.8) | copy-start | bytes 1572868
  44.4 4.6 %copy-start.2 = (bf16[32,32,32,128]{3,0,2,1:T(8,128)(2,1)}, bf16[32,32,32,128]{3,0,2,1:T(8,128)(2,1)S(1)}, u32[]{:S(2)}) copy-start(bf16[32,32,32,128]{3,0,2,1:T(8,128)(2,1)S(1)} %get-tuple-element.5) | copy-start | bytes 25165828
  44.4 5.9 %copy-start.3 = (bf16[32,32,32,128]{3,0,2,1:T(8,128)(2,1)}, bf16[32,32,32,128]{3,0,2,1:T(8,128)(2,1)S(1)}, u32[]{:S(2)}) copy-start(bf16[32,32,32,128]{3,0,2,1:T(8,128)(2,1)S(1)} %get-tuple-element.4) | copy-start | bytes 25165828
  44.4 2.3 copy-start.9
  46.7 5.8 %copy-start.6 = (f32[8,128,128]{2,1,0:T(8,128)S(1)}, f32[8,128,128]{2,1,0:T(8,128)}, u32[]{:S(2)}) copy-start(f32[8,128,128]{2,1,0:T(8,128)} %param.10) | copy-start | bytes 1572868
  46.7 6.9 %copy-start.8 = (bf16[2,32,32,128]{3,2,1,0:T(8,128)(2,1)S(1)}, bf16[2,32,32,128]{3,2,1,0:T(8,128)(2,1)}, u32[]{:S(2)}) copy-start(bf16[2,32,32,128]{3,2,1,0:T(8,128)(2,1)} %get-tuple-element.8) | copy-start | bytes 1572868
  53.5 44.9 %copy-start.13 = (f32[32]{0:T(128)S(1)}, f32[32]{0:T(128)}, u32[]{:S(2)}) copy-start(f32[32]{0:T(128)} %param.16) | copy-start | bytes 388
  93.3 28.5 %all-to-all-start.1 = ((bf16[2,1,4,2,8,4096]{5,4,3,0,1,2:T(8,128)(2,1)}), bf16[2,1,4,2,8,4096]{5,4,3,0,1,2:T(8,128)(2,1)S(1)}, u32[]{:S(2)}, u32[]{:S(2)}) async-start(bf16[2,1,4,2,8,4096]{5,4,3,0,1,2:T(8,128)(2,1)} %reshape.427), calls=%async_computation.1 | async-start | bytes 2097152 | tf_op jit(solution)/shard_map/all_to_all | solution.py:105
  137.0 18.7 %all-to-all-start.2 = ((bf16[2,1,1,2,8,128,128]{6,4,0,3,2,1,5:T(8,128)(2,1)}), bf16[2,1,1,2,8,128,128]{6,4,0,3,2,1,5:T(8,128)(2,1)S(1)}, u32[]{:S(2)}, u32[]{:S(2)}) async-start(bf16[2,1,1,2,8,128,128]{6,4,0,3,2,1,5:T(8,128)(2,1)} %copy.79), calls=%async_computation.2 | async-start | bytes 2097152 | tf_op jit(solution)/shard_map/all_to_all | solution.py:133
  163.2 17.0 %copy-start.10 = (bf16[1,128,2,128]{3,1,2,0:T(8,128)(2,1)S(1)}, bf16[1,128,2,128]{3,1,2,0:T(8,128)(2,1)}, u32[]{:S(2)}) copy-start(bf16[1,128,2,128]{3,1,2,0:T(8,128)(2,1)} %get-tuple-element.12) | copy-start | bytes 196612
  163.2 17.0 %copy-start.11 = (bf16[1,128,2,128]{3,1,2,0:T(8,128)(2,1)S(1)}, bf16[1,128,2,128]{3,1,2,0:T(8,128)(2,1)}, u32[]{:S(2)}) copy-start(bf16[1,128,2,128]{3,1,2,0:T(8,128)(2,1)} %get-tuple-element.15) | copy-start | bytes 196612
  175.6 40.1 %all-to-all-start.3 = ((bf16[4,2,65536]{2,1,0:T(2,128)(2,1)}), bf16[4,2,65536]{2,1,0:T(2,128)(2,1)}, u32[]{:S(2)}, u32[]{:S(2)}) async-start(bf16[4,2,65536]{2,1,0:T(2,128)(2,1)} %reshape.429), calls=%async_computation.3 | async-start | bytes 2097152 | tf_op jit(solution)/shard_map/all_to_all | solution.py:132
  179.8 34.0 %all-reduce.2.cloned.1.call-start = ((), (), s32[]{:S(2)}) async-start(), calls=%async_computation.4 | async-start | bytes 524288 | tf_op jit(solution)/shard_map/psum | solution.py:123
  180.4 9.3 %copy-start.4 = (f32[2,8,128,128]{2,3,1,0:T(8,128)S(1)}, f32[2,8,128,128]{2,3,1,0:T(8,128)}, u32[]{:S(2)}) copy-start(f32[2,8,128,128]{2,3,1,0:T(8,128)} %get-tuple-element.6) | copy-start | bytes 3145732
  180.4 9.3 %copy-start.12 = (f32[2]{0:T(128)S(1)}, f32[2]{0:T(128)}, u32[]{:S(2)}) copy-start(f32[2]{0:T(128)} %param.17) | copy-start | bytes 28
  191.7 39.6 %copy-start.5 = (f32[2,32,32,128]{3,2,1,0:T(8,128)S(1)}, f32[2,32,32,128]{3,2,1,0:T(8,128)}, u32[]{:S(2)}) copy-start(f32[2,32,32,128]{3,2,1,0:T(8,128)} %copy_subtract_fusion) | copy-start | bytes 3145732
  231.3 6.5 %copy-start.1 = (bf16[4,32,32,128]{3,2,1,0:T(8,128)(2,1)S(1)}, bf16[4,32,32,128]{3,2,1,0:T(8,128)(2,1)}, u32[]{:S(2)}) copy-start(bf16[4,32,32,128]{3,2,1,0:T(8,128)(2,1)} %param.12) | copy-start | bytes 3145732
Sparse Core Ops, SparseCore 0:
  190.7 23.0 all-reduce.1
where the time goes:
time: 247 us; the launch traced here: 245 us
  matrix products  61.6 us (25%)
  local copies, waits for them, and re-layouts  60 us (24%)
  waiting for transfers between devices  48.8 us (20%)
  blocking collectives  31.6 us (13%)
  starting transfers between devices  17.7 us (7%)
  between operations  14.3 us (6%)
  other arithmetic  10.5 us (4%)
    psum x1, blocking collectives, shards(): intersections = lax.psum(partial_intersections, ('gy', 'gz'))  31.6 us
    psum x1, waiting for transfers between devices, shards(): lax.psum(partial_density.astype(jnp.bfloat16), 'band').astype(jnp.float32)  22.1 us
    unnamed x37, local copies, waits for them, and re-layouts  21.8 us
    all_to_all x1, waiting for transfers between devices, shards(): lax.all_to_all(lax.all_to_all(spread, 'gy', split_axis=1, concat_axis=5,...  18.8 us
    dot_general x1, matrix products, projector_parts(): jnp.einsum('bc,cyzx->byzx', kind_hot, channels, preferred_element_type=jn...  13.7 us
    all_to_all x1, local copies, waits for them, and re-layouts, shards(): lax.all_to_all(lax.all_to_all(folded, 'gy', split_axis=5, concat_axis=1,...  10.4 us
    reshape x2, local copies, waits for them, and re-layouts, shards(): spread.reshape(orbit_count, parts_y, parts_z, 2, thin_x, rows_y * rows_z)  10.2 us
    all_to_all x1, waiting for transfers between devices, shards(): lax.all_to_all(folded, 'gy', split_axis=5, concat_axis=1, tiled=True)  7.89 us
  transfers between devices with their start and end apart: 5, of which 3 were waited for; matrix products, arithmetic and copies ran while one was open for 23% of the time, Pallas kernels for 0%

commit v1 on v0

v1 whole, which is shorter than its diff:
```python
import functools
import math

import jax
import jax.numpy as jnp
import ml_dtypes
import numpy as np
from jax import lax
from jax.experimental import pallas as pl
from jax.experimental.pallas import tpu as pltpu
from jax.sharding import PartitionSpec as P

kinetic_scale = 1.0 / 1024.0
MESH = pl.DeviceIdType.MESH
F32 = jnp.float32
BF16 = jnp.bfloat16


def dot(a, b, dims):
    return lax.dot_general(a, b, (dims, ((), ())), preferred_element_type=F32)


def parts_of(length, sign_value):
    index = np.arange(length)
    angle = 2.0 * np.pi / length * (index[:, None] * index[None, :] % length)
    cosine = np.cos(angle) / math.sqrt(length)
    sine = sign_value * np.sin(angle) / math.sqrt(length)
    return cosine, sine


def tables(length, rows_z, parts_z):
    group = length // rows_z
    same = np.eye(group)
    out = []
    for sign in (1.0, -1.0):
        c, s = parts_of(length, sign)
        square = np.block([[c, -s], [s, c]])
        out.append(square)
    inv_sq, fwd_sq = out
    order = np.arange(2 * length).reshape(2, length // 8, 8).transpose(1, 0, 2).reshape(-1)
    inv_x = inv_sq[order]
    fwd_x = fwd_sq.T[order]
    c, s = parts_of(length, 1.0)
    z_in = [
        np.einsum("wqz,jk->qjzkw", t.reshape(length, parts_z, rows_z), same).reshape(
            parts_z * group * rows_z, group * length
        )
        for t in (c, s)
    ]
    c, s = parts_of(length, -1.0)
    z_out = [
        np.einsum("qzw,jk->jwqkz", t.reshape(parts_z, rows_z, length), same).reshape(
            group * length, parts_z * group * rows_z
        )
        for t in (c, s)
    ]
    made = (inv_x, np.concatenate(z_in, 1), inv_sq, fwd_sq, np.concatenate(z_out, 1), fwd_x)
    return [np.asarray(t, dtype=np.float32).astype(ml_dtypes.bfloat16) for t in made]


def kernel(
    sizes,
    orb_ref,
    mask_ref,
    pot_ref,
    chan_ref,
    pos_ref,
    posx_ref,
    match_ref,
    occ_ref,
    ix_ref,
    tz_ref,
    t2_ref,
    f2_ref,
    tb_ref,
    fx_ref,
    out_ref,
    dens_out_ref,
    masked,
    tx,
    rx,
    tx2,
    rx2,
    zs,
    dens,
    dens_rx,
    extra,
    phase,
    fold,
    over_tx,
    over_rx,
    send_sem,
    recv_sem,
    over_send,
    over_recv,
    dens_send,
    dens_recv,
):
    N, C, A, length, rows_y, rows_z, py, pz, bands = sizes
    L = 2 * C * N * A
    half = L // 2
    group = length // rows_z
    G = rows_y // group
    S = py * pz
    cols = rows_y * rows_z
    gy = lax.axis_index("gy")
    gz = lax.axis_index("gz")
    band = lax.axis_index("band")
    me = gy * pz + gz

    def peer(d):
        to = lax.rem(me + d, S)
        return to, {"gy": to // pz, "gz": lax.rem(to, pz)}

    barrier = pltpu.get_barrier_semaphore()

    def greet(d, c):
        pl.semaphore_signal(barrier, inc=1, device_id=peer(d)[1], device_id_type=MESH)
        return c

    def greet_band(d, c):
        pl.semaphore_signal(
            barrier, inc=1, device_id={"band": lax.rem(band + d, bands)}, device_id_type=MESH
        )
        return c

    lax.fori_loop(1, S, greet, 0)
    lax.fori_loop(1, bands, greet_band, 0)

    def block_copy(src, dst, step, n, to, place, slot):
        return pltpu.make_async_remote_copy(
            src_ref=src.at[to, n],
            dst_ref=dst.at[slot, n],
            send_sem=send_sem.at[step, n, to],
            recv_sem=recv_sem.at[step, n, slot],
            device_id=place,
            device_id_type=MESH,
        )

    def send_blocks(src, dst, step, n):
        def one(d, c):
            to, place = peer(d)
            block_copy(src, dst, step, n, to, place, me).start()
            return c

        lax.fori_loop(1, S, one, 0)
        dst[me, n] = src[me, n]

    def wait_blocks(src, dst, step, n):
        def one(d, c):
            frm, place = peer(d)
            block_copy(src, dst, step, n, frm, place, frm).wait_recv()
            return c

        lax.fori_loop(1, S, one, 0)

    def wait_sent(src, dst, step, n):
        def one(d, c):
            to, place = peer(d)
            block_copy(src, dst, step, n, to, place, me).wait_send()
            return c

        lax.fori_loop(1, S, one, 0)

    def x_group(n, g, c):
        rows = pl.ds(pl.multiple_of((n * G + g) * 128, 128), 128)
        keep = mask_ref[pl.ds(pl.multiple_of(g * 128, 128), 128), :] != 0
        keep = jnp.concatenate([keep.astype(F32)] * 2, axis=1) != 0
        block = jnp.where(keep, orb_ref[rows, :].astype(F32), 0.0).astype(BF16)
        masked[rows, :] = block
        made = dot(ix_ref[...], block, ((1,), (1,))).astype(BF16)
        tx[:, n, g] = made.reshape(S, 16, 128)
        return c

    for n in range(N):
        lax.fori_loop(0, G, functools.partial(x_group, n), 0)
        if n == 0:
            pl.semaphore_wait(barrier, S - 1 + bands - 1)
        send_blocks(tx, rx, 0, n)

    def centred(index):
        return jnp.where(index >= length // 2, index - length, index).astype(F32)

    def turn(amount):
        angle = (2.0 * math.pi) * (amount - jnp.round(amount))
        return jnp.cos(angle), jnp.sin(angle)

    fy = centred(lax.broadcasted_iota(jnp.int32, (rows_y, L), 0) + gy * rows_y)
    fz = centred(lax.broadcasted_iota(jnp.int32, (rows_z, L), 0) + gz * rows_z)
    fx = centred(lax.broadcasted_iota(jnp.int32, (L, length), 1))
    cy, sy = turn(fy * pos_ref[1:2, :])
    cz, sz = turn(fz * pos_ref[2:3, :])
    cx, sx = turn(fx * posx_ref[...])
    for y in range(rows_y):
        at = pl.ds(y * rows_z, rows_z)
        phase[0, at, :] = cy[y : y + 1] * cz - sy[y : y + 1] * sz
        phase[1, at, :] = sy[y : y + 1] * cz + cy[y : y + 1] * sz
    row = lax.broadcasted_iota(jnp.int32, (L, 2 * length), 0)
    pair = lax.rem(row, half) // A
    real_row = row < half
    cs = jnp.concatenate([cx, -sx], axis=1)
    sc = jnp.concatenate([sx, cx], axis=1)
    wave = jnp.where(real_row, cs, sc)
    for i in range(C * N):
        fold[i] = jnp.where(pair == i, wave, 0.0).astype(BF16)
    lane = lax.broadcasted_iota(jnp.int32, (1, L), 1)
    sign = jnp.where(lane < half, -1.0, 1.0)

    def over_group(g, total):
        at = pl.ds(pl.multiple_of(g * 128, 128), 128)
        found = jnp.zeros((128, L), F32)
        for c in range(C):
            profile = chan_ref[c, at, :]
            profile = jnp.concatenate([profile, profile], axis=1)
            for n in range(N):
                rows = pl.ds(pl.multiple_of(n * cols + g * 128, 128), 128)
                found = found + dot(profile * masked[rows, :], fold[c * N + n], ((1,), (1,)))
        swapped = pltpu.roll(found, half, 1)
        value = phase[0, at, :] * found + sign * (phase[1, at, :] * swapped)
        return total + jnp.sum(value, axis=0, keepdims=True)

    total = lax.fori_loop(0, G, over_group, jnp.zeros((1, L), F32))
    over_tx[...] = jnp.broadcast_to(total, (8, L))

    def over_copy(to, place, slot):
        return pltpu.make_async_remote_copy(
            src_ref=over_tx,
            dst_ref=over_rx.at[slot],
            send_sem=over_send.at[to],
            recv_sem=over_recv.at[slot],
            device_id=place,
            device_id_type=MESH,
        )

    def over_start(d, c):
        to, place = peer(d)
        over_copy(to, place, me).start()
        return c

    lax.fori_loop(1, S, over_start, 0)
    over_rx[me] = over_tx[...]

    for n in range(N):
        wait_blocks(tx, rx, 0, n)

        def z_in(q, c):
            lhs = jnp.concatenate(
                [rx[q * pz + k, n].reshape(G * 16, 128) for k in range(pz)], axis=1
            )
            made = dot(lhs, tz_ref[...], ((1,), (0,)))
            u = made[:, : group * length].reshape(G, 2, 8, group * length)
            v = made[:, group * length :].reshape(G, 2, 8, group * length)
            re = u[:, 0] - v[:, 1]
            im = v[:, 0] + u[:, 1]
            for g in range(G):
                for j in range(group):
                    at = pl.multiple_of((q * rows_y + g * group + j) * 16, 16)
                    zs[pl.ds(at, 8), :] = re[g, :, j * length : (j + 1) * length]
                    zs[pl.ds(at + 8, 8), :] = im[g, :, j * length : (j + 1) * length]
            return c

        lax.fori_loop(0, py, z_in, 0)
        for x in range(8):
            low = pl.ds(x, length, stride=16)
            high = pl.ds(x + 8, length, stride=16)
            both = jnp.concatenate([zs[low, :], zs[high, :]], axis=0).astype(BF16)
            field = dot(t2_ref[...], both, ((1,), (0,)))
            re, im = field[:length], field[length:]
            weight = occ_ref[n] * (re * re + im * im)
            if n == 0:
                dens[x] = weight
            else:
                dens[x] = dens[x] + weight
            pot = pot_ref[x]
            scaled = jnp.concatenate([pot * re, pot * im], axis=0).astype(BF16)
            back = dot(f2_ref[...], scaled, ((1,), (0,)))
            zs[low, :] = back[:length]
            zs[high, :] = back[length:]

        def z_out(q, c):
            at = pl.ds(pl.multiple_of(q * rows_y * 16, 512), rows_y * 16)
            block = zs[at, :].reshape(G, group, 16, length)
            lhs = jnp.concatenate(
                [block[:, j].reshape(G * 16, length) for j in range(group)], axis=1
            ).astype(BF16)
            made = dot(lhs, tb_ref[...], ((1,), (0,)))
            u = made[:, : pz * 128].reshape(G, 2, 8, pz * 128)
            v = made[:, pz * 128 :].reshape(G, 2, 8, pz * 128)
            re = u[:, 0] - v[:, 1]
            im = v[:, 0] + u[:, 1]
            joined = jnp.concatenate([re, im], axis=1).astype(BF16)
            for k in range(pz):
                tx2[q * pz + k, n] = joined[:, :, k * 128 : (k + 1) * 128]
            return c

        lax.fori_loop(0, py, z_out, 0)
        send_blocks(tx2, rx2, 1, n)

    dens_rx[band] = dens[...].astype(BF16)

    def dens_copy(d, slot):
        to = lax.rem(band + d, bands)
        return pltpu.make_async_remote_copy(
            src_ref=dens_rx.at[band],
            dst_ref=dens_rx.at[slot],
            send_sem=dens_send.at[to],
            recv_sem=dens_recv.at[slot],
            device_id={"band": to},
            device_id_type=MESH,
        )

    def dens_start(d, c):
        dens_copy(d, band).start()
        return c

    lax.fori_loop(1, bands, dens_start, 0)

    def over_wait(d, c):
        frm, place = peer(d)
        over_copy(frm, place, frm).wait_recv()
        return c

    lax.fori_loop(1, S, over_wait, 0)
    meet = over_rx[0]
    for s in range(1, S):
        meet = meet + over_rx[s]
    terms = (match_ref[...] * meet[0:1]).astype(BF16).astype(F32)
    coef = jnp.sum(terms, axis=0, keepdims=True)
    coef_swapped = pltpu.roll(jnp.broadcast_to(coef, (8, L)), half, 1)[0:1]

    def apply_group(g, c):
        at = pl.ds(pl.multiple_of(g * 128, 128), 128)
        lhs = phase[0, at, :] * coef - phase[1, at, :] * (sign * coef_swapped)
        lhs = lhs.astype(BF16)
        index = lax.broadcasted_iota(jnp.int32, (128, length), 0) + g * 128
        ky = centred(gy * rows_y + index // rows_z)
        kz = centred(gz * rows_z + lax.rem(index, rows_z))
        kx = centred(lax.broadcasted_iota(jnp.int32, (128, length), 1))
        energy = (kinetic_scale * 0.5) * (ky * ky + kz * kz + kx * kx)
        energy = jnp.concatenate([energy, energy], axis=1)
        sums = [None] * N
        for n in range(N):
            rows = pl.ds(pl.multiple_of(n * cols + g * 128, 128), 128)
            sums[n] = energy * masked[rows, :].astype(F32)
        for k in range(C):
            profile = chan_ref[k, at, :].astype(F32)
            profile = jnp.concatenate([profile, profile], axis=1)
            for n in range(N):
                sums[n] = sums[n] + profile * dot(lhs, fold[k * N + n], ((1,), (0,)))
        for n in range(N):
            rows = pl.ds(pl.multiple_of(n * cols + g * 128, 128), 128)
            extra[rows, :] = sums[n]
        return c

    lax.fori_loop(0, G, apply_group, 0)

    def dens_wait(d, c):
        dens_copy(d, lax.rem(band + d, bands)).wait_recv()
        return c

    lax.fori_loop(1, bands, dens_wait, 0)
    whole = dens_rx[0].astype(F32)
    for b in range(1, bands):
        whole = whole + dens_rx[b].astype(F32)
    dens_out_ref[...] = whole

    for n in range(N):
        wait_blocks(tx2, rx2, 1, n)

        def finish(g, c):
            rows = pl.ds(pl.multiple_of((n * G + g) * 128, 128), 128)
            keep = mask_ref[pl.ds(pl.multiple_of(g * 128, 128), 128), :] != 0
            keep = jnp.concatenate([keep.astype(F32)] * 2, axis=1) != 0
            block = rx2[:, n, g].reshape(S * 16, 128)
            local = dot(block, fx_ref[...], ((0,), (0,)))
            out_ref[rows, :] = jnp.where(keep, local + extra[rows, :], 0.0).astype(BF16)
            return c

        lax.fori_loop(0, G, finish, 0)

    for n in range(N):
        wait_sent(tx, rx, 0, n)
        wait_sent(tx2, rx2, 1, n)

    def over_done(d, c):
        to, place = peer(d)
        over_copy(to, place, me).wait_send()
        return c

    lax.fori_loop(1, S, over_done, 0)

    def dens_done(d, c):
        dens_copy(d, band).wait_send()
        return c

    lax.fori_loop(1, bands, dens_done, 0)


def shards(
    orbitals,
    potential,
    cutoff_mask,
    channels,
    positions,
    proj_atom,
    proj_chan,
    coupling,
    occupations,
):
    N, rows_y, rows_z, wide = orbitals.shape
    length = wide // 2
    C = channels.shape[0]
    A = positions.shape[0]
    py, pz, bands = lax.axis_size("gy"), lax.axis_size("gz"), lax.axis_size("band")
    S = py * pz
    L = 2 * C * N * A
    G = rows_y * rows_z // 128
    cols = rows_y * rows_z
    made = [jnp.asarray(t) for t in tables(length, rows_z, pz)]
    lanes = jnp.arange(L, dtype=jnp.int32)
    lane_chan = lanes % (L // 2) // (N * A)
    lane_atom = lanes % A
    same = (proj_chan[:, None] == lane_chan[None]) & (proj_atom[:, None] == lane_atom[None])
    match = jnp.where(same, coupling[:, None], 0.0)
    tiled = jnp.tile(positions, (L // A, 1))
    vmem = pl.BlockSpec(memory_space=pltpu.VMEM)
    smem = pl.BlockSpec(memory_space=pltpu.SMEM)
    sizes = (N, C, A, length, rows_y, rows_z, py, pz, bands)
    planes = (S, N, G, 16, 128)
    applied, density = pl.pallas_call(
        functools.partial(kernel, sizes),
        out_shape=(
            jax.ShapeDtypeStruct((N * cols, wide), BF16),
            jax.ShapeDtypeStruct(potential.shape, F32),
        ),
        in_specs=[vmem] * 7 + [smem] + [vmem] * 6,
        out_specs=(vmem, vmem),
        scratch_shapes=[
            pltpu.VMEM((N * cols, wide), BF16),
            pltpu.VMEM(planes, BF16),
            pltpu.VMEM(planes, BF16),
            pltpu.VMEM(planes, BF16),
            pltpu.VMEM(planes, BF16),
            pltpu.VMEM((length * 16, length), F32),
            pltpu.VMEM(potential.shape, F32),
            pltpu.VMEM((bands,) + potential.shape, BF16),
            pltpu.VMEM((N * cols, wide), F32),
            pltpu.VMEM((2, cols, L), F32),
            pltpu.VMEM((C * N, L, wide), BF16),
            pltpu.VMEM((8, L), F32),
            pltpu.VMEM((S, 8, L), F32),
            pltpu.SemaphoreType.DMA((2, N, S)),
            pltpu.SemaphoreType.DMA((2, N, S)),
            pltpu.SemaphoreType.DMA((S,)),
            pltpu.SemaphoreType.DMA((S,)),
            pltpu.SemaphoreType.DMA((bands,)),
            pltpu.SemaphoreType.DMA((bands,)),
        ],
        compiler_params=pltpu.CompilerParams(
            collective_id=0, has_side_effects=True, vmem_limit_bytes=56 * 1024 * 1024
        ),
    )(
        orbitals.reshape(N * cols, wide),
        cutoff_mask.reshape(cols, length),
        potential,
        channels.reshape(C, cols, length),
        tiled.T,
        tiled[:, 0:1],
        match,
        occupations,
        *made,
    )
    return (applied.reshape(orbitals.shape), density)


def solution(mesh):
    placed = (
        P("band", "gy", "gz", None),
        P(("gy", "gz"), None, None),
        P("gy", "gz", None),
        P(None, "gy", "gz", None),
        P(),
        P(),
        P(),
        P(),
        P("band"),
    )
    return jax.shard_map(
        shards,
        mesh=mesh,
        in_specs=placed,
        out_specs=(P("band", "gy", "gz", None), P(("gy", "gz"), None, None)),
        check_vma=False,
    )
```

time: 247 us -> 68.6 us (0.28)
  matrix products: 61.6 us -> 0 us
  Pallas kernels: 0 us -> 60.7 us
  local copies, waits for them, and re-layouts: 60 us -> 5.76 us
  waiting for transfers between devices: 48.8 us -> 0 us
  blocking collectives: 31.6 us -> 0 us
  starting transfers between devices: 17.7 us -> 0 us
  between operations: 14.3 us -> 0.67 us
  other arithmetic: 10.5 us -> 0.69 us
    dot_general x15 -> x0, matrix products: 61.6 us -> none  [the longest x1 13.7 us: projector_parts(): jnp.einsum('bc,cyzx->byzx', kind_hot, channels, preferred_element_type=jn...]
    pallas_call x0 -> x1, Pallas kernels: none -> 60.7 us  [shards(): pl.pallas_call(functools.partial(kernel, sizes), out_shape=(jax.ShapeDtyp...]
    psum x1 -> x0, blocking collectives: 31.6 us -> none  [shards(): intersections = lax.psum(partial_intersections, ('gy', 'gz'))]
    all_to_all x4 -> x0, waiting for transfers between devices: 26.7 us -> none  [the longest x1 18.8 us: shards(): lax.all_to_all(lax.all_to_all(spread, 'gy', split_axis=1, concat_axis=5,...]
    psum x1 -> x0, waiting for transfers between devices: 22.1 us -> none  [shards(): lax.psum(partial_density.astype(jnp.bfloat16), 'band').astype(jnp.float32)]
    all_to_all x4 -> x0, local copies, waits for them, and re-layouts: 20.3 us -> none  [the longest x1 10.4 us: shards(): lax.all_to_all(lax.all_to_all(folded, 'gy', split_axis=5, concat_axis=1,...]
    all_to_all x4 -> x0, starting transfers between devices: 17.4 us -> none  [the longest x1 5.13 us: shards(): lax.all_to_all(folded, 'gy', split_axis=5, concat_axis=1, tiled=True)]
    unnamed x37 -> x13, local copies, waits for them, and re-layouts: 21.8 us -> 4.48 us
  transfers between devices with their start and end apart: 5 -> 0, of which waited for: 3 -> 0; matrix products, arithmetic and copies ran while one was open for 23% -> 0% of each run, Pallas kernels for 0% -> 0%
where the time goes in v1:
time: 68.6 us; the launch traced here: 67.8 us
  Pallas kernels  60.7 us (88%)
  local copies, waits for them, and re-layouts  5.76 us (8%)
  other arithmetic  0.69 us (1%)
    pallas_call x1, Pallas kernels, shards(): pl.pallas_call(functools.partial(kernel, sizes), out_shape=(jax.ShapeDtyp...  60.7 us
    unnamed x13, local copies, waits for them, and re-layouts  4.48 us

profile of v1, /device:TPU:1, one launch (start us, length us, event | category | flops | bytes accessed | tf_op | source)
XLA Modules:
  0.0 67.8 jit_solution(3674518414981313816)
XLA Ops:
  0.6 0.0 copy-start.1
  0.7 0.7 copy-done.1
  1.3 0.0 copy-start.2
  1.3 0.0 copy-start.3
  1.3 0.0 copy-start.4
  1.3 0.1 copy.17
  1.4 0.6 copy-done.2
  2.0 0.0 copy-done.3
  2.0 0.0 copy-done.4
  2.0 0.7 %and_select_fusion.match_ref = f32[32,128]{1,0:T(8,128)} fusion(f32[32]{0:T(128)S(1)} %copy-done.2, s32[128]{0:T(128)S(1)} %get-tuple-element.8, s32[128]{0:T(128)S(1)} %get-tuple-element.9, s32[32]{0:T(128)S(1)} %copy-done.3, s32[32]{0:T(128)S(1)} %copy-done.4), kind=kLoop, calls=%fused_computation.2 | loop fusion | flops 16384 | bytes 17792 | tf_op jit(solution)/shard_map/jit(_where)/select_n | solution.py:424
  2.7 0.6 broadcast_bitcast_fusion.1
  3.3 0.6 copy.18.pos_ref
  4.0 60.7 %shard_map.158 = (bf16[2048,256]{1,0:T(8,128)(2,1)}, f32[8,128,128]{2,1,0:T(8,128)}) custom-call(bf16[2048,256]{1,0:T(8,128)(2,1)} %bitcast.11, s32[1024,128]{1,0:T(8,128)} %bitcast.13, f32[8,128,128]{2,1,0:T(8,128)} %pot_ref.1, bf16[4,1024,128]{2,1,0:T(8,128)(2,1)} %bitcast.12, f32[3,128]{1,0:T(4,128)} %copy.18.pos_ref, f32[128,1]{1,0:T(8,128)} %bitcast.14, ...), custom_call_target="tpu_custom_call" | custom-call | tf_op jit(solution)/shard_map/pallas_call | solution.py:430
  64.7 0.0 copy-start
  64.7 2.3 %copy.21 = bf16[2,32,32,256]{3,2,1,0:T(8,128)(2,1)} copy(bf16[2,32,32,256]{3,2,1,0:T(8,128)(2,1)} %bitcast.10) | data formatting | bytes 2097152
  67.0 0.0 copy-done
  67.0 0.8 %copy.22 = f32[8,128,128]{2,1,0:T(8,128)} copy(f32[8,128,128]{2,1,0:T(8,128)S(1)} %copy-done) | data formatting | bytes 1048576
  (1 shorter events, 0.0 us)
Async XLA Ops:
  0.6 0.7 %copy-start.1 = (f32[8,3]{0,1:T(4,128)S(1)}, f32[8,3]{0,1:T(4,128)}, u32[]{:S(2)}) copy-start(f32[8,3]{0,1:T(4,128)} %param.19) | copy-start | bytes 292
  1.3 0.7 copy-start.2
  1.3 0.7 copy-start.3
  1.3 0.7 %copy-start.4 = (s32[32]{0:T(128)S(1)}, s32[32]{0:T(128)}, u32[]{:S(2)}) copy-start(s32[32]{0:T(128)} %param.21) | copy-start | bytes 388
  64.7 2.3 %copy-start = (f32[8,128,128]{2,1,0:T(8,128)S(1)}, f32[8,128,128]{2,1,0:T(8,128)}, u32[]{:S(2)}) copy-start(f32[8,128,128]{2,1,0:T(8,128)} %get-tuple-element.13) | copy-start | bytes 1572868

commit v2 on v1

--- a/solution.py
+++ b/solution.py
@@ -60,22 +60,37 @@
 
 def kernel(
     sizes,
+    pos_ref,
+    atom_ref,
+    kind_ref,
+    coup_ref,
+    occ_ref,
+    orb_hbm,
+    mask_hbm,
+    ix_hbm,
+    chan_hbm,
+    tz_hbm,
+    t2_hbm,
+    pot_hbm,
+    f2_hbm,
+    tb_hbm,
+    fx_hbm,
+    out_hbm,
+    dens_hbm,
     orb_ref,
     mask_ref,
-    pot_ref,
+    ix_ref,
     chan_ref,
-    pos_ref,
-    posx_ref,
-    match_ref,
-    occ_ref,
-    ix_ref,
     tz_ref,
     t2_ref,
+    pot_ref,
     f2_ref,
     tb_ref,
     fx_ref,
     out_ref,
     dens_out_ref,
+    in_sem,
+    out_sem,
     masked,
     tx,
     rx,
@@ -108,9 +123,41 @@
     band = lax.axis_index("band")
     me = gy * pz + gz
 
+    half_rows = cols
+    moves = [
+        pltpu.make_async_copy(
+            orb_hbm.at[pl.ds(n * half_rows, half_rows)],
+            orb_ref.at[pl.ds(n * half_rows, half_rows)],
+            in_sem.at[n],
+        )
+        for n in range(N)
+    ]
+    held = (
+        (ix_hbm, ix_ref),
+        (mask_hbm, mask_ref),
+        (chan_hbm, chan_ref),
+        (tz_hbm, tz_ref),
+        (t2_hbm, t2_ref),
+        (pot_hbm, pot_ref),
+        (f2_hbm, f2_ref),
+        (tb_hbm, tb_ref),
+        (fx_hbm, fx_ref),
+    )
+    loads = [pltpu.make_async_copy(a, b, in_sem.at[N + i]) for i, (a, b) in enumerate(held)]
+    for move in loads[:2] + moves + loads[2:]:
+        move.start()
+
     def peer(d):
         to = lax.rem(me + d, S)
         return to, {"gy": to // pz, "gz": lax.rem(to, pz)}
+
+    def place_of(to_y, to_z):
+        return to_y * pz + to_z, {"gy": to_y, "gz": to_z}
+
+    if pz == 4:
+        far = [lax.rem(gz + 2, pz), 3 - gz, gz + 1 - 2 * lax.rem(gz, 2)]
+    else:
+        far = [lax.rem(gz + k, pz) for k in range(1, pz)]
 
     barrier = pltpu.get_barrier_semaphore()
 
@@ -138,12 +185,14 @@
         )
 
     def send_blocks(src, dst, step, n):
-        def one(d, c):
-            to, place = peer(d)
-            block_copy(src, dst, step, n, to, place, me).start()
-            return c
-
-        lax.fori_loop(1, S, one, 0)
+        for to_z in far + [gz]:
+
+            def one(d, c):
+                to, place = place_of(lax.rem(gy + d, py), to_z)
+                block_copy(src, dst, step, n, to, place, me).start()
+                return c
+
+            lax.fori_loop(1 if to_z is gz else 0, py, one, 0)
         dst[me, n] = src[me, n]
 
     def wait_blocks(src, dst, step, n):
@@ -172,7 +221,10 @@
         tx[:, n, g] = made.reshape(S, 16, 128)
         return c
 
+    loads[0].wait()
+    loads[1].wait()
     for n in range(N):
+        moves[n].wait()
         lax.fori_loop(0, G, functools.partial(x_group, n), 0)
         if n == 0:
             pl.semaphore_wait(barrier, S - 1 + bands - 1)
@@ -188,9 +240,20 @@
     fy = centred(lax.broadcasted_iota(jnp.int32, (rows_y, L), 0) + gy * rows_y)
     fz = centred(lax.broadcasted_iota(jnp.int32, (rows_z, L), 0) + gz * rows_z)
     fx = centred(lax.broadcasted_iota(jnp.int32, (L, length), 1))
-    cy, sy = turn(fy * pos_ref[1:2, :])
-    cz, sz = turn(fz * pos_ref[2:3, :])
-    cx, sx = turn(fx * posx_ref[...])
+    lane = lax.broadcasted_iota(jnp.int32, (1, L), 1)
+    lane_atom = lax.rem(lane, A)
+    lane_chan = lax.rem(lane, half) // (N * A)
+    row_atom = lax.rem(lax.broadcasted_iota(jnp.int32, (L, length), 0), A)
+    at_x = jnp.zeros((L, length), F32)
+    at_y = jnp.zeros((1, L), F32)
+    at_z = jnp.zeros((1, L), F32)
+    for a in range(A):
+        at_x = jnp.where(row_atom == a, pos_ref[0, a], at_x)
+        at_y = jnp.where(lane_atom == a, pos_ref[1, a], at_y)
+        at_z = jnp.where(lane_atom == a, pos_ref[2, a], at_z)
+    cy, sy = turn(fy * at_y)
+    cz, sz = turn(fz * at_z)
+    cx, sx = turn(fx * at_x)
     for y in range(rows_y):
         at = pl.ds(y * rows_z, rows_z)
         phase[0, at, :] = cy[y : y + 1] * cz - sy[y : y + 1] * sz
@@ -203,8 +266,9 @@
     wave = jnp.where(real_row, cs, sc)
     for i in range(C * N):
         fold[i] = jnp.where(pair == i, wave, 0.0).astype(BF16)
-    lane = lax.broadcasted_iota(jnp.int32, (1, L), 1)
     sign = jnp.where(lane < half, -1.0, 1.0)
+
+    loads[2].wait()
 
     def over_group(g, total):
         at = pl.ds(pl.multiple_of(g * 128, 128), 128)
@@ -240,6 +304,8 @@
     lax.fori_loop(1, S, over_start, 0)
     over_rx[me] = over_tx[...]
 
+    for move in loads[3:]:
+        move.wait()
     for n in range(N):
         wait_blocks(tx, rx, 0, n)
 
@@ -324,8 +390,11 @@
     meet = over_rx[0]
     for s in range(1, S):
         meet = meet + over_rx[s]
-    terms = (match_ref[...] * meet[0:1]).astype(BF16).astype(F32)
-    coef = jnp.sum(terms, axis=0, keepdims=True)
+    meet = meet[0:1]
+    coef = jnp.zeros((1, L), F32)
+    for p in range(coup_ref.shape[0]):
+        hit = (lane_chan == kind_ref[p]) & (lane_atom == atom_ref[p])
+        coef = coef + jnp.where(hit, (coup_ref[p] * meet).astype(BF16).astype(F32), 0.0)
     coef_swapped = pltpu.roll(jnp.broadcast_to(coef, (8, L)), half, 1)[0:1]
 
     def apply_group(g, c):
@@ -363,7 +432,10 @@
     for b in range(1, bands):
         whole = whole + dens_rx[b].astype(F32)
     dens_out_ref[...] = whole
-
+    dens_move = pltpu.make_async_copy(dens_out_ref, dens_hbm, out_sem.at[N])
+    dens_move.start()
+
+    leaves = []
     for n in range(N):
         wait_blocks(tx2, rx2, 1, n)
 
@@ -377,6 +449,10 @@
             return c
 
         lax.fori_loop(0, G, finish, 0)
+        span = pl.ds(n * half_rows, half_rows)
+        leave = pltpu.make_async_copy(out_ref.at[span], out_hbm.at[span], out_sem.at[n])
+        leave.start()
+        leaves.append(leave)
 
     for n in range(N):
         wait_sent(tx, rx, 0, n)
@@ -394,6 +470,25 @@
         return c
 
     lax.fori_loop(1, bands, dens_done, 0)
+    dens_move.wait()
+    for leave in leaves:
+        leave.wait()
+
+
+def hand_on(pieces, *refs):
+    count = len(refs) // 2
+    sem = refs[-1]
+    moves = []
+    for i in range(count):
+        src, dst = refs[i], refs[count + i]
+        rows = src.shape[0] // pieces
+        for k in range(pieces):
+            span = pl.ds(k * rows, rows)
+            moves.append(pltpu.make_async_copy(src.at[span], dst.at[span], sem.at[i, k]))
+    for move in moves:
+        move.start()
+    for move in moves:
+        move.wait()
 
 
 def shards(
@@ -416,14 +511,8 @@
     L = 2 * C * N * A
     G = rows_y * rows_z // 128
     cols = rows_y * rows_z
-    made = [jnp.asarray(t) for t in tables(length, rows_z, pz)]
-    lanes = jnp.arange(L, dtype=jnp.int32)
-    lane_chan = lanes % (L // 2) // (N * A)
-    lane_atom = lanes % A
-    same = (proj_chan[:, None] == lane_chan[None]) & (proj_atom[:, None] == lane_atom[None])
-    match = jnp.where(same, coupling[:, None], 0.0)
-    tiled = jnp.tile(positions, (L // A, 1))
-    vmem = pl.BlockSpec(memory_space=pltpu.VMEM)
+    ix, tz, t2, f2, tb, fx = [jnp.asarray(t) for t in tables(length, rows_z, pz)]
+    hbm = pl.BlockSpec(memory_space=pl.ANY)
     smem = pl.BlockSpec(memory_space=pltpu.SMEM)
     sizes = (N, C, A, length, rows_y, rows_z, py, pz, bands)
     planes = (S, N, G, 16, 128)
@@ -433,9 +522,23 @@
             jax.ShapeDtypeStruct((N * cols, wide), BF16),
             jax.ShapeDtypeStruct(potential.shape, F32),
         ),
-        in_specs=[vmem] * 7 + [smem] + [vmem] * 6,
-        out_specs=(vmem, vmem),
+        in_specs=[smem] * 5 + [hbm] * 10,
+        out_specs=(hbm, hbm),
         scratch_shapes=[
+            pltpu.VMEM((N * cols, wide), BF16),
+            pltpu.VMEM((cols, length), jnp.int32),
+            pltpu.VMEM(ix.shape, BF16),
+            pltpu.VMEM((C, cols, length), BF16),
+            pltpu.VMEM(tz.shape, BF16),
+            pltpu.VMEM(t2.shape, BF16),
+            pltpu.VMEM(potential.shape, F32),
+            pltpu.VMEM(f2.shape, BF16),
+            pltpu.VMEM(tb.shape, BF16),
+            pltpu.VMEM(fx.shape, BF16),
+            pltpu.VMEM((N * cols, wide), BF16),
+            pltpu.VMEM(potential.shape, F32),
+            pltpu.SemaphoreType.DMA((N + 9,)),
+            pltpu.SemaphoreType.DMA((N + 1,)),
             pltpu.VMEM((N * cols, wide), BF16),
             pltpu.VMEM(planes, BF16),
             pltpu.VMEM(planes, BF16),
@@ -460,16 +563,33 @@
             collective_id=0, has_side_effects=True, vmem_limit_bytes=56 * 1024 * 1024
         ),
     )(
+        positions.T,
+        proj_atom,
+        proj_chan,
+        coupling,
+        occupations,
         orbitals.reshape(N * cols, wide),
         cutoff_mask.reshape(cols, length),
+        ix,
+        channels.reshape(C, cols, length),
+        tz,
+        t2,
         potential,
-        channels.reshape(C, cols, length),
-        tiled.T,
-        tiled[:, 0:1],
-        match,
-        occupations,
-        *made,
+        f2,
+        tb,
+        fx,
     )
+    pieces = 4
+    applied, density = pl.pallas_call(
+        functools.partial(hand_on, pieces),
+        out_shape=(
+            jax.ShapeDtypeStruct((N * cols, wide), BF16),
+            jax.ShapeDtypeStruct(potential.shape, F32),
+        ),
+        in_specs=[hbm] * 2,
+        out_specs=(hbm, hbm),
+        scratch_shapes=[pltpu.SemaphoreType.DMA((2, pieces))],
+    )(applied, density)
     return (applied.reshape(orbitals.shape), density)
 
 

time: 68.6 us -> 107 us (1.56)
  Pallas kernels: 60.7 us -> 106 us
  local copies, waits for them, and re-layouts: 5.76 us -> 0 us
    pallas_call x0 -> x1, Pallas kernels: none -> 48.8 us  [shards(): pl.pallas_call(functools.partial(hand_on, pieces), out_shape=(jax.ShapeDt...]
    unnamed x13 -> x0, local copies, waits for them, and re-layouts: 4.48 us -> none
    pallas_call x1, Pallas kernels: 60.7 us -> 57.4 us  [shards(): pl.pallas_call(functools.partial(kernel, sizes), out_shape=(jax.ShapeDtyp...]
where the time goes in v2:
time: 107 us
  Pallas kernels  106 us (99%)
    pallas_call x1, Pallas kernels, shards(): pl.pallas_call(functools.partial(kernel, sizes), out_shape=(jax.ShapeDtyp...  57.4 us
    pallas_call x1, Pallas kernels, shards(): pl.pallas_call(functools.partial(hand_on, pieces), out_shape=(jax.ShapeDt...  48.8 us

profile of v2, /device:TPU:1, one launch (start us, length us, event | category | flops | bytes accessed | tf_op | source)
XLA Modules:
  0.0 106.8 jit_solution(8352445970326067155)
XLA Ops:
  0.6 57.4 %shard_map.158 = (bf16[2048,256]{1,0:T(8,128)(2,1)}, f32[8,128,128]{2,1,0:T(8,128)}) custom-call(f32[3,8]{1,0:T(4,128)} %bitcast.8, s32[32]{0:T(128)} %atom_ref.1, s32[32]{0:T(128)} %kind_ref.1, f32[32]{0:T(128)} %coup_ref.1, f32[2]{0:T(128)} %occ_ref.1, bf16[2048,256]{1,0:T(8,128)(2,1)} %bitcast.5, s32[1024,128]{1,0:T(8,128)} %bitcast.7, ...), custom_call_target="tpu_custom_call" | custom-call | tf_op jit(solution)/shard_map/pallas_call | solution.py:519
  58.0 48.8 %shard_map.159 = (bf16[2048,256]{1,0:T(8,128)(2,1)}, f32[8,128,128]{2,1,0:T(8,128)}) custom-call(bf16[2048,256]{1,0:T(8,128)(2,1)} %get-tuple-element.6.refs_0_, f32[8,128,128]{2,1,0:T(8,128)} %get-tuple-element.7.refs_1_), custom_call_target="tpu_custom_call" | custom-call | tf_op jit(solution)/shard_map/pallas_call | solution.py:583

commit v3 on v2

--- a/solution.py
+++ b/solution.py
@@ -56,6 +56,27 @@
     ]
     made = (inv_x, np.concatenate(z_in, 1), inv_sq, fwd_sq, np.concatenate(z_out, 1), fwd_x)
     return [np.asarray(t, dtype=np.float32).astype(ml_dtypes.bfloat16) for t in made]
+
+
+def folds(length, rows):
+    group = length // rows
+    count = rows // group
+    first = np.arange(rows) + length // 4
+    inside = first[:, None] ** 2 + first[None, :] ** 2 < (length // 2) ** 2
+    width = inside.reshape(count, group, rows).any(axis=1).sum(axis=1)
+    kept = [g for g in range(count) if width[g]]
+    plan = []
+    while kept:
+        g = kept.pop(0)
+        other = None
+        for h in reversed(kept):
+            if width[g] + width[h] <= rows:
+                other = h
+                kept.remove(h)
+                break
+        plan.append((g, other, int(width[g])))
+    dropped = [g for g in range(count) if not width[g]]
+    return plan, dropped
 
 
 def kernel(
@@ -96,6 +117,10 @@
     rx,
     tx2,
     rx2,
+    txc,
+    rxc,
+    txc2,
+    rxc2,
     zs,
     dens,
     dens_rx,
@@ -174,7 +199,30 @@
     lax.fori_loop(1, S, greet, 0)
     lax.fori_loop(1, bands, greet_band, 0)
 
-    def block_copy(src, dst, step, n, to, place, slot):
+    plan, dropped = folds(length, rows_y)
+    corner = [k for k in range(pz) if 0 < k < pz - 1]
+
+    def middle(k, parts):
+        return (k > 0) & (k < parts - 1)
+
+    def is_corner(y, z):
+        return middle(y, py) & middle(z, pz)
+
+    def place_in(t, y):
+        return jnp.where(y >= py // 2, G - 1 - t, t)
+
+    def shifted(block, amount, flip):
+        return pltpu.roll(block, (128 - amount) % 128 if flip else amount % 128, 1)
+
+    def depth_in(shape, flip):
+        z = lax.rem(lax.broadcasted_iota(jnp.int32, shape, 1), rows_z)
+        return rows_z - 1 - z if flip else z
+
+    wide_bufs = ((tx, rx), (tx2, rx2))
+    slim_bufs = ((txc, rxc), (txc2, rxc2))
+
+    def block_copy(slim, step, n, to, place, slot):
+        src, dst = (slim_bufs if slim else wide_bufs)[step]
         return pltpu.make_async_remote_copy(
             src_ref=src.at[to, n],
             dst_ref=dst.at[slot, n],
@@ -184,32 +232,97 @@
             device_id_type=MESH,
         )
 
-    def send_blocks(src, dst, step, n):
+    def by_kind(slim, act):
+        pl.when(slim)(lambda: act(True))
+        pl.when(jnp.logical_not(slim))(lambda: act(False))
+
+    def send_row(step, n, d):
+        to_y = lax.rem(gy + d, py)
         for to_z in far + [gz]:
-
-            def one(d, c):
-                to, place = place_of(lax.rem(gy + d, py), to_z)
-                block_copy(src, dst, step, n, to, place, me).start()
-                return c
-
-            lax.fori_loop(1 if to_z is gz else 0, py, one, 0)
-        dst[me, n] = src[me, n]
-
-    def wait_blocks(src, dst, step, n):
-        def one(d, c):
-            frm, place = peer(d)
-            block_copy(src, dst, step, n, frm, place, frm).wait_recv()
-            return c
-
-        lax.fori_loop(1, S, one, 0)
-
-    def wait_sent(src, dst, step, n):
+            to, place = place_of(to_y, to_z)
+            slim = is_corner(gy, gz) if step == 0 else is_corner(to_y, to_z)
+
+            def start():
+                by_kind(slim, lambda k: block_copy(k, step, n, to, place, me).start())
+
+            if to_z is gz:
+                pl.when(d > 0)(start)
+            else:
+                start()
+
+    def wait_row(step, n, d):
+        from_y = lax.rem(gy + py - d, py)
+        for from_z in far + [gz]:
+            frm, place = place_of(from_y, from_z)
+            slim = is_corner(from_y, from_z) if step == 0 else is_corner(gy, gz)
+
+            def wait():
+                by_kind(slim, lambda k: block_copy(k, step, n, frm, place, frm).wait_recv())
+
+            if from_z is gz:
+                pl.when(d > 0)(wait)
+            else:
+                wait()
+
+    def wait_sent(step, n):
         def one(d, c):
             to, place = peer(d)
-            block_copy(src, dst, step, n, to, place, me).wait_send()
+            to_y, to_z = place["gy"], place["gz"]
+            slim = is_corner(gy, gz) if step == 0 else is_corner(to_y, to_z)
+            by_kind(slim, lambda k: block_copy(k, step, n, to, place, me).wait_send())
             return c
 
         lax.fori_loop(1, S, one, 0)
+
+    def fold_mine(n):
+        for t, (g, other, width) in enumerate(plan):
+            block = tx[:, n, place_in(g, gy)].astype(F32).reshape(S * 16, 128)
+            if other is not None:
+                more = tx[:, n, place_in(other, gy)].astype(F32).reshape(S * 16, 128)
+                block = block + jnp.where(
+                    gz >= pz // 2, shifted(more, width, True), shifted(more, width, False)
+                )
+            txc[:, n, t] = block.astype(BF16).reshape(S, 16, 128)
+
+    def unfold_from(n, y, k):
+        s = y * pz + k
+        flip = k >= pz // 2
+        depth = depth_in((16, 128), flip)
+        for t, (g, other, width) in enumerate(plan):
+            block = rxc[s, n, t].astype(F32)
+            if other is None:
+                rx[s, n, place_in(g, y)] = block.astype(BF16)
+            else:
+                rx[s, n, place_in(g, y)] = jnp.where(depth < width, block, 0.0).astype(BF16)
+                more = shifted(block, width, not flip)
+                more = jnp.where(depth < rows_z - width, more, 0.0)
+                rx[s, n, place_in(other, y)] = more.astype(BF16)
+        for g in dropped:
+            rx[s, n, place_in(g, y)] = jnp.zeros((16, 128), BF16)
+
+    def fold_for(n, y, k):
+        s = y * pz + k
+        flip = k >= pz // 2
+        depth = depth_in((16, 128), flip)
+        for t, (g, other, width) in enumerate(plan):
+            block = tx2[s, n, place_in(g, y)].astype(F32)
+            if other is not None:
+                more = shifted(tx2[s, n, place_in(other, y)].astype(F32), width, flip)
+                block = jnp.where(depth < width, block, more)
+            txc2[s, n, t] = block.astype(BF16)
+
+    def unfold_mine(n):
+        for t, (g, other, width) in enumerate(plan):
+            block = rxc2[:, n, t]
+            rx2[:, n, place_in(g, gy)] = block
+            if other is not None:
+                block = block.astype(F32).reshape(S * 16, 128)
+                more = jnp.where(
+                    gz >= pz // 2, shifted(block, width, False), shifted(block, width, True)
+                )
+                rx2[:, n, place_in(other, gy)] = more.astype(BF16).reshape(S, 16, 128)
+        for g in dropped:
+            rx2[:, n, place_in(g, gy)] = jnp.zeros((S, 16, 128), BF16)
 
     def x_group(n, g, c):
         rows = pl.ds(pl.multiple_of((n * G + g) * 128, 128), 128)
@@ -228,7 +341,14 @@
         lax.fori_loop(0, G, functools.partial(x_group, n), 0)
         if n == 0:
             pl.semaphore_wait(barrier, S - 1 + bands - 1)
-        send_blocks(tx, rx, 0, n)
+        pl.when(is_corner(gy, gz))(functools.partial(fold_mine, n))
+
+        def send_all(d, c):
+            send_row(0, n, d)
+            return c
+
+        lax.fori_loop(0, py, send_all, 0)
+        rx[me, n] = tx[me, n]
 
     def centred(index):
         return jnp.where(index >= length // 2, index - length, index).astype(F32)
@@ -307,9 +427,14 @@
     for move in loads[3:]:
         move.wait()
     for n in range(N):
-        wait_blocks(tx, rx, 0, n)
-
-        def z_in(q, c):
+
+        def z_in(d, c):
+            wait_row(0, n, d)
+            q = lax.rem(gy + py - d, py)
+            for k in corner:
+                pl.when(middle(q, py) & (q * pz + k != me))(
+                    functools.partial(unfold_from, n, q, k)
+                )
             lhs = jnp.concatenate(
                 [rx[q * pz + k, n].reshape(G * 16, 128) for k in range(pz)], axis=1
             )
@@ -343,7 +468,8 @@
             zs[low, :] = back[:length]
             zs[high, :] = back[length:]
 
-        def z_out(q, c):
+        def z_out(d, c):
+            q = lax.rem(gy + d, py)
             at = pl.ds(pl.multiple_of(q * rows_y * 16, 512), rows_y * 16)
             block = zs[at, :].reshape(G, group, 16, length)
             lhs = jnp.concatenate(
@@ -357,10 +483,20 @@
             joined = jnp.concatenate([re, im], axis=1).astype(BF16)
             for k in range(pz):
                 tx2[q * pz + k, n] = joined[:, :, k * 128 : (k + 1) * 128]
+            for k in corner:
+                pl.when(middle(q, py))(functools.partial(fold_for, n, q, k))
+            send_row(1, n, d)
             return c
 
         lax.fori_loop(0, py, z_out, 0)
-        send_blocks(tx2, rx2, 1, n)
+
+        @pl.when(is_corner(gy, gz))
+        def _():
+            rxc2[me, n] = txc2[me, n]
+
+        @pl.when(jnp.logical_not(is_corner(gy, gz)))
+        def _():
+            rx2[me, n] = tx2[me, n]
 
     dens_rx[band] = dens[...].astype(BF16)
 
@@ -437,7 +573,12 @@
 
     leaves = []
     for n in range(N):
-        wait_blocks(tx2, rx2, 1, n)
+        def arrive(d, c):
+            wait_row(1, n, d)
+            return c
+
+        lax.fori_loop(0, py, arrive, 0)
+        pl.when(is_corner(gy, gz))(functools.partial(unfold_mine, n))
 
         def finish(g, c):
             rows = pl.ds(pl.multiple_of((n * G + g) * 128, 128), 128)
@@ -455,8 +596,8 @@
         leaves.append(leave)
 
     for n in range(N):
-        wait_sent(tx, rx, 0, n)
-        wait_sent(tx2, rx2, 1, n)
+        wait_sent(0, n)
+        wait_sent(1, n)
 
     def over_done(d, c):
         to, place = peer(d)
@@ -476,19 +617,27 @@
 
 
 def hand_on(pieces, *refs):
-    count = len(refs) // 2
-    sem = refs[-1]
-    moves = []
-    for i in range(count):
-        src, dst = refs[i], refs[count + i]
-        rows = src.shape[0] // pieces
+    ins, outs, held = refs[:2], refs[2:4], refs[4:6]
+    sem_in, sem_out = refs[6:]
+    steps = []
+    for i in range(2):
+        rows = ins[i].shape[0] // pieces
         for k in range(pieces):
             span = pl.ds(k * rows, rows)
-            moves.append(pltpu.make_async_copy(src.at[span], dst.at[span], sem.at[i, k]))
-    for move in moves:
-        move.start()
-    for move in moves:
-        move.wait()
+            here = held[i].at[span]
+            steps.append(
+                (
+                    pltpu.make_async_copy(ins[i].at[span], here, sem_in.at[i, k]),
+                    pltpu.make_async_copy(here, outs[i].at[span], sem_out.at[i, k]),
+                )
+            )
+    for read, _ in steps:
+        read.start()
+    for read, write in steps:
+        read.wait()
+        write.start()
+    for _, write in steps:
+        write.wait()
 
 
 def shards(
@@ -516,6 +665,7 @@
     smem = pl.BlockSpec(memory_space=pltpu.SMEM)
     sizes = (N, C, A, length, rows_y, rows_z, py, pz, bands)
     planes = (S, N, G, 16, 128)
+    slim = (S, N, len(folds(length, rows_y)[0]), 16, 128)
     applied, density = pl.pallas_call(
         functools.partial(kernel, sizes),
         out_shape=(
@@ -544,6 +694,10 @@
             pltpu.VMEM(planes, BF16),
             pltpu.VMEM(planes, BF16),
             pltpu.VMEM(planes, BF16),
+            pltpu.VMEM(slim, BF16),
+            pltpu.VMEM(slim, BF16),
+            pltpu.VMEM(slim, BF16),
+            pltpu.VMEM(slim, BF16),
             pltpu.VMEM((length * 16, length), F32),
             pltpu.VMEM(potential.shape, F32),
             pltpu.VMEM((bands,) + potential.shape, BF16),
@@ -588,7 +742,12 @@
         ),
         in_specs=[hbm] * 2,
         out_specs=(hbm, hbm),
-        scratch_shapes=[pltpu.SemaphoreType.DMA((2, pieces))],
+        scratch_shapes=[
+            pltpu.VMEM((N * cols, wide), BF16),
+            pltpu.VMEM(potential.shape, F32),
+            pltpu.SemaphoreType.DMA((2, pieces)),
+            pltpu.SemaphoreType.DMA((2, pieces)),
+        ],
     )(applied, density)
     return (applied.reshape(orbitals.shape), density)
 

time: 107 us -> 59.8 us (0.56)
  Pallas kernels: 106 us -> 59 us
    pallas_call x1, Pallas kernels: 48.8 us -> 2.22 us  [shards(): pl.pallas_call(functools.partial(hand_on, pieces), out_shape=(jax.ShapeDt...]
where the time goes in v3:
time: 59.8 us; the launch traced here: 59.6 us
  Pallas kernels  59 us (99%)
  between operations  0.64 us (1%)
    pallas_call x1, Pallas kernels, shards(): pl.pallas_call(functools.partial(kernel, sizes), out_shape=(jax.ShapeDtyp...  56.7 us
    pallas_call x1, Pallas kernels, shards(): pl.pallas_call(functools.partial(hand_on, pieces), out_shape=(jax.ShapeDt...  2.22 us

profile of v3, /device:TPU:1, one launch (start us, length us, event | category | flops | bytes accessed | tf_op | source)
XLA Modules:
  0.0 59.6 jit_solution(14216990454083771693)
XLA Ops:
  0.6 56.7 %shard_map.158 = (bf16[2048,256]{1,0:T(8,128)(2,1)}, f32[8,128,128]{2,1,0:T(8,128)}) custom-call(f32[3,8]{1,0:T(4,128)} %bitcast.8, s32[32]{0:T(128)} %atom_ref.1, s32[32]{0:T(128)} %kind_ref.1, f32[32]{0:T(128)} %coup_ref.1, f32[2]{0:T(128)} %occ_ref.1, bf16[2048,256]{1,0:T(8,128)(2,1)} %bitcast.5, s32[1024,128]{1,0:T(8,128)} %bitcast.7, ...), custom_call_target="tpu_custom_call" | custom-call | tf_op jit(solution)/shard_map/pallas_call | solution.py:669
  57.4 2.2 %shard_map.159 = (bf16[2048,256]{1,0:T(8,128)(2,1)}, f32[8,128,128]{2,1,0:T(8,128)}) custom-call(bf16[2048,256]{1,0:T(8,128)(2,1)} %get-tuple-element.6.refs_0_, f32[8,128,128]{2,1,0:T(8,128)} %get-tuple-element.7.refs_1_), custom_call_target="tpu_custom_call" | custom-call | tf_op jit(solution)/shard_map/pallas_call | solution.py:737

commit v4 on v3

--- a/solution.py
+++ b/solution.py
@@ -127,6 +127,8 @@
     extra,
     phase,
     fold,
+    foldt,
+    weighed,
     over_tx,
     over_rx,
     send_sem,
@@ -324,21 +326,23 @@
         for g in dropped:
             rx2[:, n, place_in(g, gy)] = jnp.zeros((S, 16, 128), BF16)
 
-    def x_group(n, g, c):
-        rows = pl.ds(pl.multiple_of((n * G + g) * 128, 128), 128)
-        keep = mask_ref[pl.ds(pl.multiple_of(g * 128, 128), 128), :] != 0
-        keep = jnp.concatenate([keep.astype(F32)] * 2, axis=1) != 0
-        block = jnp.where(keep, orb_ref[rows, :].astype(F32), 0.0).astype(BF16)
-        masked[rows, :] = block
-        made = dot(ix_ref[...], block, ((1,), (1,))).astype(BF16)
-        tx[:, n, g] = made.reshape(S, 16, 128)
+    def x_group(n, h, c):
+        rows = pl.ds(pl.multiple_of(n * cols + h * 256, 256), 256)
+        keep = mask_ref[pl.ds(pl.multiple_of(h * 256, 256), 256), :] != 0
+        for part in range(2):
+            span = pl.ds(part * length, length)
+            block = jnp.where(keep, orb_ref[rows, span].astype(F32), 0.0)
+            masked[rows, span] = block.astype(BF16)
+        made = dot(ix_ref[...], masked[rows, :], ((1,), (1,))).astype(BF16)
+        tx[:, n, 2 * h] = made[:, :128].reshape(S, 16, 128)
+        tx[:, n, 2 * h + 1] = made[:, 128:].reshape(S, 16, 128)
         return c
 
     loads[0].wait()
     loads[1].wait()
     for n in range(N):
         moves[n].wait()
-        lax.fori_loop(0, G, functools.partial(x_group, n), 0)
+        lax.fori_loop(0, G // 2, functools.partial(x_group, n), 0)
         if n == 0:
             pl.semaphore_wait(barrier, S - 1 + bands - 1)
         pl.when(is_corner(gy, gz))(functools.partial(fold_mine, n))
@@ -354,8 +358,23 @@
         return jnp.where(index >= length // 2, index - length, index).astype(F32)
 
     def turn(amount):
-        angle = (2.0 * math.pi) * (amount - jnp.round(amount))
-        return jnp.cos(angle), jnp.sin(angle)
+        quarter = jnp.round(amount * 4.0)
+        rest = (2.0 * math.pi) * (amount - 0.25 * quarter)
+        sq = rest * rest
+        cosine = 1.0 + sq * (
+            -0.5 + sq * (1.0 / 24 + sq * (-1.0 / 720 + sq * (1.0 / 40320 - sq * (1.0 / 3628800))))
+        )
+        sine = rest * (
+            1.0
+            + sq * (-1.0 / 6 + sq * (1.0 / 120 + sq * (-1.0 / 5040 + sq * (1.0 / 362880))))
+        )
+        left = quarter - 4.0 * jnp.floor(quarter * 0.25)
+        odd = (left == 1.0) | (left == 3.0)
+        first = jnp.where(odd, sine, cosine)
+        second = jnp.where(odd, cosine, sine)
+        first = jnp.where((left == 1.0) | (left == 2.0), -first, first)
+        second = jnp.where(left >= 2.0, -second, second)
+        return first, second
 
     fy = centred(lax.broadcasted_iota(jnp.int32, (rows_y, L), 0) + gy * rows_y)
     fz = centred(lax.broadcasted_iota(jnp.int32, (rows_z, L), 0) + gz * rows_z)
@@ -378,32 +397,35 @@
         at = pl.ds(y * rows_z, rows_z)
         phase[0, at, :] = cy[y : y + 1] * cz - sy[y : y + 1] * sz
         phase[1, at, :] = sy[y : y + 1] * cz + cy[y : y + 1] * sz
-    row = lax.broadcasted_iota(jnp.int32, (L, 2 * length), 0)
+    row = lax.broadcasted_iota(jnp.int32, (L, length), 0)
     pair = lax.rem(row, half) // A
-    real_row = row < half
-    cs = jnp.concatenate([cx, -sx], axis=1)
-    sc = jnp.concatenate([sx, cx], axis=1)
-    wave = jnp.where(real_row, cs, sc)
-    for i in range(C * N):
-        fold[i] = jnp.where(pair == i, wave, 0.0).astype(BF16)
+    waves = (jnp.where(row < half, cx, sx), jnp.where(row < half, -sx, cx))
+    lane_pair = lax.rem(lax.broadcasted_iota(jnp.int32, (length, L), 1), half) // A
+    for part in range(2):
+        turned = waves[part].T
+        for i in range(C * N):
+            at = i * 2 * length + part * length
+            fold[:, pl.ds(at, length)] = jnp.where(pair == i, waves[part], 0.0).astype(BF16)
+            foldt[pl.ds(at, length), :] = jnp.where(lane_pair == i, turned, 0.0).astype(BF16)
     sign = jnp.where(lane < half, -1.0, 1.0)
 
     loads[2].wait()
 
-    def over_group(g, total):
-        at = pl.ds(pl.multiple_of(g * 128, 128), 128)
-        found = jnp.zeros((128, L), F32)
+    def over_group(h, total):
+        at = pl.ds(pl.multiple_of(h * 256, 256), 256)
         for c in range(C):
             profile = chan_ref[c, at, :]
-            profile = jnp.concatenate([profile, profile], axis=1)
             for n in range(N):
-                rows = pl.ds(pl.multiple_of(n * cols + g * 128, 128), 128)
-                found = found + dot(profile * masked[rows, :], fold[c * N + n], ((1,), (1,)))
+                rows = pl.ds(pl.multiple_of(n * cols + h * 256, 256), 256)
+                for part in range(2):
+                    lanes = pl.ds(((c * N + n) * 2 + part) * length, length)
+                    weighed[:, lanes] = profile * masked[rows, pl.ds(part * length, length)]
+        found = dot(weighed[...], foldt[...], ((1,), (0,)))
         swapped = pltpu.roll(found, half, 1)
         value = phase[0, at, :] * found + sign * (phase[1, at, :] * swapped)
         return total + jnp.sum(value, axis=0, keepdims=True)
 
-    total = lax.fori_loop(0, G, over_group, jnp.zeros((1, L), F32))
+    total = lax.fori_loop(0, G // 2, over_group, jnp.zeros((1, L), F32))
     over_tx[...] = jnp.broadcast_to(total, (8, L))
 
     def over_copy(to, place, slot):
@@ -451,22 +473,26 @@
             return c
 
         lax.fori_loop(0, py, z_in, 0)
-        for x in range(8):
-            low = pl.ds(x, length, stride=16)
-            high = pl.ds(x + 8, length, stride=16)
-            both = jnp.concatenate([zs[low, :], zs[high, :]], axis=0).astype(BF16)
+        for x in range(0, 8, 2):
+            spans = [pl.ds(x + i, length, stride=16) for i in (0, 1, 8, 9)]
+            got = [zs[span, :] for span in spans]
+            both = jnp.concatenate(
+                [jnp.concatenate(got[:2], axis=1), jnp.concatenate(got[2:], axis=1)], axis=0
+            ).astype(BF16)
             field = dot(t2_ref[...], both, ((1,), (0,)))
-            re, im = field[:length], field[length:]
-            weight = occ_ref[n] * (re * re + im * im)
-            if n == 0:
-                dens[x] = weight
-            else:
-                dens[x] = dens[x] + weight
-            pot = pot_ref[x]
-            scaled = jnp.concatenate([pot * re, pot * im], axis=0).astype(BF16)
-            back = dot(f2_ref[...], scaled, ((1,), (0,)))
-            zs[low, :] = back[:length]
-            zs[high, :] = back[length:]
+            ends = []
+            for i in range(2):
+                lanes = slice(i * length, (i + 1) * length)
+                re, im = field[:length, lanes], field[length:, lanes]
+                weight = occ_ref[n] * (re * re + im * im)
+                dens[x + i] = weight if n == 0 else dens[x + i] + weight
+                pot = pot_ref[x + i]
+                ends.append(jnp.concatenate([pot * re, pot * im], axis=0).astype(BF16))
+            back = dot(f2_ref[...], jnp.concatenate(ends, axis=1), ((1,), (0,)))
+            zs[spans[0], :] = back[:length, :length]
+            zs[spans[1], :] = back[:length, length:]
+            zs[spans[2], :] = back[length:, :length]
+            zs[spans[3], :] = back[length:, length:]
 
         def z_out(d, c):
             q = lax.rem(gy + d, py)
@@ -533,31 +559,33 @@
         coef = coef + jnp.where(hit, (coup_ref[p] * meet).astype(BF16).astype(F32), 0.0)
     coef_swapped = pltpu.roll(jnp.broadcast_to(coef, (8, L)), half, 1)[0:1]
 
-    def apply_group(g, c):
-        at = pl.ds(pl.multiple_of(g * 128, 128), 128)
+    def apply_group(h, c):
+        at = pl.ds(pl.multiple_of(h * 256, 256), 256)
         lhs = phase[0, at, :] * coef - phase[1, at, :] * (sign * coef_swapped)
         lhs = lhs.astype(BF16)
-        index = lax.broadcasted_iota(jnp.int32, (128, length), 0) + g * 128
+        index = lax.broadcasted_iota(jnp.int32, (256, length), 0) + h * 256
         ky = centred(gy * rows_y + index // rows_z)
         kz = centred(gz * rows_z + lax.rem(index, rows_z))
-        kx = centred(lax.broadcasted_iota(jnp.int32, (128, length), 1))
+        kx = centred(lax.broadcasted_iota(jnp.int32, (256, length), 1))
         energy = (kinetic_scale * 0.5) * (ky * ky + kz * kz + kx * kx)
-        energy = jnp.concatenate([energy, energy], axis=1)
-        sums = [None] * N
         for n in range(N):
-            rows = pl.ds(pl.multiple_of(n * cols + g * 128, 128), 128)
-            sums[n] = energy * masked[rows, :].astype(F32)
-        for k in range(C):
-            profile = chan_ref[k, at, :].astype(F32)
-            profile = jnp.concatenate([profile, profile], axis=1)
-            for n in range(N):
-                sums[n] = sums[n] + profile * dot(lhs, fold[k * N + n], ((1,), (0,)))
-        for n in range(N):
-            rows = pl.ds(pl.multiple_of(n * cols + g * 128, 128), 128)
-            extra[rows, :] = sums[n]
-        return c
-
-    lax.fori_loop(0, G, apply_group, 0)
+            rows = pl.ds(pl.multiple_of(n * cols + h * 256, 256), 256)
+            parts = [
+                energy * masked[rows, pl.ds(part * length, length)].astype(F32)
+                for part in range(2)
+            ]
+            for k in range(C):
+                profile = chan_ref[k, at, :].astype(F32)
+                made = dot(
+                    lhs, fold[:, pl.ds((k * N + n) * 2 * length, 2 * length)], ((1,), (0,))
+                )
+                parts[0] = parts[0] + profile * made[:, :length]
+                parts[1] = parts[1] + profile * made[:, length:]
+            for part in range(2):
+                extra[rows, pl.ds(part * length, length)] = parts[part]
+        return c
+
+    lax.fori_loop(0, G // 2, apply_group, 0)
 
     def dens_wait(d, c):
         dens_copy(d, lax.rem(band + d, bands)).wait_recv()
@@ -580,16 +608,20 @@
         lax.fori_loop(0, py, arrive, 0)
         pl.when(is_corner(gy, gz))(functools.partial(unfold_mine, n))
 
-        def finish(g, c):
-            rows = pl.ds(pl.multiple_of((n * G + g) * 128, 128), 128)
-            keep = mask_ref[pl.ds(pl.multiple_of(g * 128, 128), 128), :] != 0
-            keep = jnp.concatenate([keep.astype(F32)] * 2, axis=1) != 0
-            block = rx2[:, n, g].reshape(S * 16, 128)
+        def finish(h, c):
+            rows = pl.ds(pl.multiple_of(n * cols + h * 256, 256), 256)
+            keep = mask_ref[pl.ds(pl.multiple_of(h * 256, 256), 256), :] != 0
+            block = jnp.concatenate(
+                [rx2[:, n, 2 * h + i].reshape(S * 16, 128) for i in range(2)], axis=1
+            )
             local = dot(block, fx_ref[...], ((0,), (0,)))
-            out_ref[rows, :] = jnp.where(keep, local + extra[rows, :], 0.0).astype(BF16)
+            for part in range(2):
+                lanes = pl.ds(part * length, length)
+                value = local[:, part * length : (part + 1) * length] + extra[rows, lanes]
+                out_ref[rows, lanes] = jnp.where(keep, value, 0.0).astype(BF16)
             return c
 
-        lax.fori_loop(0, G, finish, 0)
+        lax.fori_loop(0, G // 2, finish, 0)
         span = pl.ds(n * half_rows, half_rows)
         leave = pltpu.make_async_copy(out_ref.at[span], out_hbm.at[span], out_sem.at[n])
         leave.start()
@@ -703,7 +735,9 @@
             pltpu.VMEM((bands,) + potential.shape, BF16),
             pltpu.VMEM((N * cols, wide), F32),
             pltpu.VMEM((2, cols, L), F32),
-            pltpu.VMEM((C * N, L, wide), BF16),
+            pltpu.VMEM((L, C * N * wide), BF16),
+            pltpu.VMEM((C * N * wide, L), BF16),
+            pltpu.VMEM((256, C * N * wide), BF16),
             pltpu.VMEM((8, L), F32),
             pltpu.VMEM((S, 8, L), F32),
             pltpu.SemaphoreType.DMA((2, N, S)),

time: 59.8 us -> 57.6 us (0.963)
  Pallas kernels: 59 us -> 56.8 us
    pallas_call x1, Pallas kernels: 56.7 us -> 54.6 us  [shards(): pl.pallas_call(functools.partial(kernel, sizes), out_shape=(jax.ShapeDtyp...]
where the time goes in v4:
time: 57.6 us; the launch traced here: 57.4 us
  Pallas kernels  56.8 us (99%)
  between operations  0.64 us (1%)
    pallas_call x1, Pallas kernels, shards(): pl.pallas_call(functools.partial(kernel, sizes), out_shape=(jax.ShapeDtyp...  54.6 us
    pallas_call x1, Pallas kernels, shards(): pl.pallas_call(functools.partial(hand_on, pieces), out_shape=(jax.ShapeDt...  2.22 us

profile of v4, /device:TPU:1, one launch (start us, length us, event | category | flops | bytes accessed | tf_op | source)
XLA Modules:
  0.0 57.4 jit_solution(16569850356061808836)
XLA Ops:
  0.6 54.6 %shard_map.158 = (bf16[2048,256]{1,0:T(8,128)(2,1)}, f32[8,128,128]{2,1,0:T(8,128)}) custom-call(f32[3,8]{1,0:T(4,128)} %bitcast.8, s32[32]{0:T(128)} %atom_ref.1, s32[32]{0:T(128)} %kind_ref.1, f32[32]{0:T(128)} %coup_ref.1, f32[2]{0:T(128)} %occ_ref.1, bf16[2048,256]{1,0:T(8,128)(2,1)} %bitcast.5, s32[1024,128]{1,0:T(8,128)} %bitcast.7, ...), custom_call_target="tpu_custom_call" | custom-call | tf_op jit(solution)/shard_map/pallas_call | solution.py:701
  55.2 2.2 %shard_map.159 = (bf16[2048,256]{1,0:T(8,128)(2,1)}, f32[8,128,128]{2,1,0:T(8,128)}) custom-call(bf16[2048,256]{1,0:T(8,128)(2,1)} %get-tuple-element.6.refs_0_, f32[8,128,128]{2,1,0:T(8,128)} %get-tuple-element.7.refs_1_), custom_call_target="tpu_custom_call" | custom-call | tf_op jit(solution)/shard_map/pallas_call | solution.py:771

commit v5 on v4

--- a/solution.py
+++ b/solution.py
@@ -171,7 +171,7 @@
         (fx_hbm, fx_ref),
     )
     loads = [pltpu.make_async_copy(a, b, in_sem.at[N + i]) for i, (a, b) in enumerate(held)]
-    for move in loads[:2] + moves + loads[2:]:
+    for move in loads[:2] + moves:
         move.start()
 
     def peer(d):
@@ -340,19 +340,24 @@
 
     loads[0].wait()
     loads[1].wait()
+    def send_first(n):
+        pl.when(is_corner(gy, gz))(functools.partial(fold_mine, n))
+
+        def send_all(d, c):
+            send_row(0, n, d)
+            return c
+
+        lax.fori_loop(0, py, send_all, 0)
+        rx[me, n] = tx[me, n]
+
     for n in range(N):
         moves[n].wait()
         lax.fori_loop(0, G // 2, functools.partial(x_group, n), 0)
         if n == 0:
             pl.semaphore_wait(barrier, S - 1 + bands - 1)
-        pl.when(is_corner(gy, gz))(functools.partial(fold_mine, n))
-
-        def send_all(d, c):
-            send_row(0, n, d)
-            return c
-
-        lax.fori_loop(0, py, send_all, 0)
-        rx[me, n] = tx[me, n]
+            send_first(0)
+            for move in loads[2:]:
+                move.start()
 
     def centred(index):
         return jnp.where(index >= length // 2, index - length, index).astype(F32)
@@ -446,6 +451,9 @@
     lax.fori_loop(1, S, over_start, 0)
     over_rx[me] = over_tx[...]
 
+    if N > 1:
+        send_first(1)
+
     for move in loads[3:]:
         move.wait()
     for n in range(N):
@@ -523,6 +531,9 @@
         @pl.when(jnp.logical_not(is_corner(gy, gz)))
         def _():
             rx2[me, n] = tx2[me, n]
+
+        if n + 2 < N:
+            send_first(n + 2)
 
     dens_rx[band] = dens[...].astype(BF16)
 
@@ -599,8 +610,24 @@
     dens_move = pltpu.make_async_copy(dens_out_ref, dens_hbm, out_sem.at[N])
     dens_move.start()
 
+    def over_done(d, c):
+        to, place = peer(d)
+        over_copy(to, place, me).wait_send()
+        return c
+
+    lax.fori_loop(1, S, over_done, 0)
+
+    def dens_done(d, c):
+        dens_copy(d, band).wait_send()
+        return c
+
+    lax.fori_loop(1, bands, dens_done, 0)
     leaves = []
     for n in range(N):
+        wait_sent(0, n)
+    for n in range(N):
+        wait_sent(1, n)
+
         def arrive(d, c):
             wait_row(1, n, d)
             return c
@@ -627,22 +654,6 @@
         leave.start()
         leaves.append(leave)
 
-    for n in range(N):
-        wait_sent(0, n)
-        wait_sent(1, n)
-
-    def over_done(d, c):
-        to, place = peer(d)
-        over_copy(to, place, me).wait_send()
-        return c
-
-    lax.fori_loop(1, S, over_done, 0)
-
-    def dens_done(d, c):
-        dens_copy(d, band).wait_send()
-        return c
-
-    lax.fori_loop(1, bands, dens_done, 0)
     dens_move.wait()
     for leave in leaves:
         leave.wait()

time: 57.6 us -> 57.4 us (level)
  no operation moved by 1% of the time
where the time goes in v5:
time: 57.4 us; the launch traced here: 57.2 us
  Pallas kernels  56.5 us (98%)
  between operations  0.64 us (1%)
    pallas_call x1, Pallas kernels, shards(): pl.pallas_call(functools.partial(kernel, sizes), out_shape=(jax.ShapeDtyp...  54.3 us
    pallas_call x1, Pallas kernels, shards(): pl.pallas_call(functools.partial(hand_on, pieces), out_shape=(jax.ShapeDt...  2.22 us

profile of v5, /device:TPU:1, one launch (start us, length us, event | category | flops | bytes accessed | tf_op | source)
XLA Modules:
  0.0 57.2 jit_solution(1119363902495167002)
XLA Ops:
  0.6 54.3 %shard_map.158 = (bf16[2048,256]{1,0:T(8,128)(2,1)}, f32[8,128,128]{2,1,0:T(8,128)}) custom-call(f32[3,8]{1,0:T(4,128)} %bitcast.8, s32[32]{0:T(128)} %atom_ref.1, s32[32]{0:T(128)} %kind_ref.1, f32[32]{0:T(128)} %coup_ref.1, f32[2]{0:T(128)} %occ_ref.1, bf16[2048,256]{1,0:T(8,128)(2,1)} %bitcast.5, s32[1024,128]{1,0:T(8,128)} %bitcast.7, ...), custom_call_target="tpu_custom_call" | custom-call | tf_op jit(solution)/shard_map/pallas_call | solution.py:712
  54.9 2.2 %shard_map.159 = (bf16[2048,256]{1,0:T(8,128)(2,1)}, f32[8,128,128]{2,1,0:T(8,128)}) custom-call(bf16[2048,256]{1,0:T(8,128)(2,1)} %get-tuple-element.6.refs_0_, f32[8,128,128]{2,1,0:T(8,128)} %get-tuple-element.7.refs_1_), custom_call_target="tpu_custom_call" | custom-call | tf_op jit(solution)/shard_map/pallas_call | solution.py:782

commit v6 on v5

--- a/solution.py
+++ b/solution.py
@@ -54,7 +54,11 @@
         )
         for t in (c, s)
     ]
-    made = (inv_x, np.concatenate(z_in, 1), inv_sq, fwd_sq, np.concatenate(z_out, 1), fwd_x)
+    z_in, z_out = (
+        np.stack([t.reshape(len(t), -1, 128) for t in pair], 2).reshape(len(pair[0]), -1)
+        for pair in (z_in, z_out)
+    )
+    made = (inv_x, z_in, inv_sq, fwd_sq, z_out, fwd_x)
     return [np.asarray(t, dtype=np.float32).astype(ml_dtypes.bfloat16) for t in made]
 
 
@@ -129,6 +133,7 @@
     fold,
     foldt,
     weighed,
+    stack,
     over_tx,
     over_rx,
     send_sem,
@@ -465,22 +470,23 @@
                 pl.when(middle(q, py) & (q * pz + k != me))(
                     functools.partial(unfold_from, n, q, k)
                 )
-            lhs = jnp.concatenate(
-                [rx[q * pz + k, n].reshape(G * 16, 128) for k in range(pz)], axis=1
-            )
-            made = dot(lhs, tz_ref[...], ((1,), (0,)))
-            u = made[:, : group * length].reshape(G, 2, 8, group * length)
-            v = made[:, group * length :].reshape(G, 2, 8, group * length)
-            re = u[:, 0] - v[:, 1]
-            im = v[:, 0] + u[:, 1]
-            for g in range(G):
-                for j in range(group):
-                    at = pl.multiple_of((q * rows_y + g * group + j) * 16, 16)
-                    zs[pl.ds(at, 8), :] = re[g, :, j * length : (j + 1) * length]
-                    zs[pl.ds(at + 8, 8), :] = im[g, :, j * length : (j + 1) * length]
             return c
 
         lax.fori_loop(0, py, z_in, 0)
+        for q in range(py):
+            for k in range(pz):
+                stack[pl.ds(q * G * 16, G * 16), pl.ds(k * 128, 128)] = rx[
+                    q * pz + k, n
+                ].reshape(G * 16, 128)
+        for j in range(group):
+            made = dot(stack[...], tz_ref[:, pl.ds(j * 256, 256)], ((1,), (0,)))
+            made = made.reshape(py * G, 2, 8, 256)
+            re = made[:, 0, :, :128] - made[:, 1, :, 128:]
+            im = made[:, 0, :, 128:] + made[:, 1, :, :128]
+            for i in range(py * G):
+                at = (i * group + j) * 16
+                zs[pl.ds(at, 8), :] = re[i]
+                zs[pl.ds(at + 8, 8), :] = im[i]
         for x in range(0, 8, 2):
             spans = [pl.ds(x + i, length, stride=16) for i in (0, 1, 8, 9)]
             got = [zs[span, :] for span in spans]
@@ -502,27 +508,37 @@
             zs[spans[2], :] = back[length:, :length]
             zs[spans[3], :] = back[length:, length:]
 
-        def z_out(d, c):
-            q = lax.rem(gy + d, py)
-            at = pl.ds(pl.multiple_of(q * rows_y * 16, 512), rows_y * 16)
-            block = zs[at, :].reshape(G, group, 16, length)
-            lhs = jnp.concatenate(
-                [block[:, j].reshape(G * 16, length) for j in range(group)], axis=1
-            ).astype(BF16)
-            made = dot(lhs, tb_ref[...], ((1,), (0,)))
-            u = made[:, : pz * 128].reshape(G, 2, 8, pz * 128)
-            v = made[:, pz * 128 :].reshape(G, 2, 8, pz * 128)
-            re = u[:, 0] - v[:, 1]
-            im = v[:, 0] + u[:, 1]
-            joined = jnp.concatenate([re, im], axis=1).astype(BF16)
-            for k in range(pz):
-                tx2[q * pz + k, n] = joined[:, :, k * 128 : (k + 1) * 128]
-            for k in corner:
-                pl.when(middle(q, py))(functools.partial(fold_for, n, q, k))
-            send_row(1, n, d)
-            return c
-
-        lax.fori_loop(0, py, z_out, 0)
+        block = zs[...].reshape(py * G, group, 16, length)
+        for j in range(group):
+            stack[:, pl.ds(j * 128, 128)] = (
+                block[:, j].reshape(py * G * 16, length).astype(BF16)
+            )
+        for k in far + [gz]:
+            span = pl.ds(pl.multiple_of(k * 256, 256), 256)
+            made = dot(stack[...], tb_ref[:, span], ((1,), (0,)))
+            made = made.reshape(py * G, 2, 8, 256)
+            re = made[:, 0, :, :128] - made[:, 1, :, 128:]
+            im = made[:, 0, :, 128:] + made[:, 1, :, :128]
+            joined = jnp.concatenate([re, im], axis=1).astype(BF16).reshape(py, G, 16, 128)
+            for q in range(py):
+                tx2[q * pz + k, n] = joined[q]
+            for fixed in corner:
+
+                @pl.when(k == fixed)
+                def _():
+                    for q in range(1, py - 1):
+                        fold_for(n, q, fixed)
+
+            def send_on(d, c):
+                to_y = lax.rem(gy + d, py)
+                to, place = place_of(to_y, k)
+                by_kind(
+                    is_corner(to_y, k),
+                    lambda kind: block_copy(kind, 1, n, to, place, me).start(),
+                )
+                return c
+
+            lax.fori_loop(1 if k is gz else 0, py, send_on, 0)
 
         @pl.when(is_corner(gy, gz))
         def _():
@@ -749,6 +765,7 @@
             pltpu.VMEM((L, C * N * wide), BF16),
             pltpu.VMEM((C * N * wide, L), BF16),
             pltpu.VMEM((256, C * N * wide), BF16),
+            pltpu.VMEM((length * 4, length * 4), BF16),
             pltpu.VMEM((8, L), F32),
             pltpu.VMEM((S, 8, L), F32),
             pltpu.SemaphoreType.DMA((2, N, S)),

time: 57.4 us -> 56.4 us (0.983)
  Pallas kernels: 56.5 us -> 55.5 us
    pallas_call x1, Pallas kernels: 54.3 us -> 53.3 us  [shards(): pl.pallas_call(functools.partial(kernel, sizes), out_shape=(jax.ShapeDtyp...]
where the time goes in v6:
time: 56.4 us; the launch traced here: 56.2 us
  Pallas kernels  55.5 us (98%)
  between operations  0.64 us (1%)
    pallas_call x1, Pallas kernels, shards(): pl.pallas_call(functools.partial(kernel, sizes), out_shape=(jax.ShapeDtyp...  53.3 us
    pallas_call x1, Pallas kernels, shards(): pl.pallas_call(functools.partial(hand_on, pieces), out_shape=(jax.ShapeDt...  2.22 us

profile of v6, /device:TPU:1, one launch (start us, length us, event | category | flops | bytes accessed | tf_op | source)
XLA Modules:
  0.0 56.2 jit_solution(1801808954390210439)
XLA Ops:
  0.6 53.3 %shard_map.158 = (bf16[2048,256]{1,0:T(8,128)(2,1)}, f32[8,128,128]{2,1,0:T(8,128)}) custom-call(f32[3,8]{1,0:T(4,128)} %bitcast.8, s32[32]{0:T(128)} %atom_ref.1, s32[32]{0:T(128)} %kind_ref.1, f32[32]{0:T(128)} %coup_ref.1, f32[2]{0:T(128)} %occ_ref.1, bf16[2048,256]{1,0:T(8,128)(2,1)} %bitcast.5, s32[1024,128]{1,0:T(8,128)} %bitcast.7, ...), custom_call_target="tpu_custom_call" | custom-call | tf_op jit(solution)/shard_map/pallas_call | solution.py:728
  54.0 2.2 %shard_map.159 = (bf16[2048,256]{1,0:T(8,128)(2,1)}, f32[8,128,128]{2,1,0:T(8,128)}) custom-call(bf16[2048,256]{1,0:T(8,128)(2,1)} %get-tuple-element.6.refs_0_, f32[8,128,128]{2,1,0:T(8,128)} %get-tuple-element.7.refs_1_), custom_call_target="tpu_custom_call" | custom-call | tf_op jit(solution)/shard_map/pallas_call | solution.py:799
